TPU v7x, 512 devices: a whole 4x4x16 slice. The times are simulated.
512 devices in a mesh: dp: 64 (over z, y), head: 8 (over x, core).
Axes of the slice: x: 4, y: 4, z: 16, core: 2. Of those that a mesh axis runs over, the one named last changes fastest.
Arguments:
- query: bfloat16 [8192, 2048], P(('dp', 'head')), may hold values from -6 to 6
- key: bfloat16 [8192, 2048], P(('dp', 'head')), may hold values from -6 to 6
- value: bfloat16 [8192, 4096], P(('dp', 'head')), may hold values from -6 to 6
- beta_logit: float32 [8192, 32], P(('dp', 'head')), may hold values from -8 to 8
- decay: float32 [8192, 32], P(('dp', 'head')), may hold values from 0 to 1
- out_grad: bfloat16 [8192, 4096], P(('dp', 'head')), may hold values from -6 to 6
- ratio: float32 [8192], P(('dp', 'head')), may hold values from 0.5 to 2
- clip_mask: int32 [8192], P(('dp', 'head')), may hold values 0 or 1
- lengths: int32 [16], replicated, may hold values from 1 to 4096, 8192 in all
Outputs:
- query_grad: bfloat16 [8192, 2048], P(('dp', 'head'))
- key_grad: bfloat16 [8192, 2048], P(('dp', 'head'))
- value_grad: bfloat16 [8192, 4096], P(('dp', 'head'))
- beta_grad: float32 [8192, 32], P(('dp', 'head'))
- decay_grad: float32 [8192, 32], P(('dp', 'head'))
Inputs may be any that keep to these rules, and one draw needn't show every extreme that they name: 16 lengths of at least 1 that sum to 8192; the longest is exactly 4096.
All inputs are finite; a program needn't handle non-finite values. No bound on the sum of `clip_mask` on one device may be relied on, other than what follows from the above.
Results may differ from a plain program's by a relative error of at most 0.0013.
Values may be sent and summed in bfloat16 or wider, within the bound.
A program may use at most 128 MiB of HBM per device.

v0:
```python
import jax
import jax.numpy as jnp
from jax import lax
from jax.sharding import PartitionSpec as P

HEAD_DIM = 128
GROUP = 64


exact_mode = lax.Precision.HIGHEST


def from_behind(block, axis, distance):
    devices = range(lax.axis_size(axis))
    route = [(i - distance, i) for i in devices if i - distance in devices]
    return lax.ppermute(block, axis, route)


def unit_rows(values):
    return values * lax.rsqrt(jnp.sum(values * values, axis=-1, keepdims=True) + 1e-06)


def segments(lengths, positions):
    doc_bounds = jnp.cumsum(lengths) - lengths
    doc_starts = jnp.any(positions[:, None] == doc_bounds[None, :], axis=1)
    doc_ids = jnp.sum((doc_bounds[None, :] <= positions[:, None]).astype(jnp.int32), axis=1)
    return (doc_starts, doc_ids)


def matmul_heads(left, right):
    return jnp.einsum("hij,hjk->hik", left, right, precision=exact_mode)


def combine(earlier, later):
    return (matmul_heads(later[0], earlier[0]), matmul_heads(later[0], earlier[1]) + later[1])


def to_blocks(values, block_count):
    return jnp.swapaxes(values.reshape((block_count, GROUP) + values.shape[1:]), 1, 2)


def group_terms(query_f, key_f, value_f, beta_logit, decay, doc_blocks, first_docs):
    tok_count = query_f.shape[0]
    block_count = tok_count // GROUP
    value_heads = value_f.shape[1] // HEAD_DIM
    q = unit_rows(query_f.reshape(tok_count, -1, HEAD_DIM)) * HEAD_DIM ** (-0.5)
    k = unit_rows(key_f.reshape(tok_count, -1, HEAD_DIM))
    repeat_count = value_heads // q.shape[1]
    q = to_blocks(jnp.repeat(q, repeat_count, axis=1), block_count)
    k = to_blocks(jnp.repeat(k, repeat_count, axis=1), block_count)
    v = to_blocks(value_f.reshape(tok_count, value_heads, HEAD_DIM), block_count)
    beta = to_blocks(jax.nn.sigmoid(beta_logit), block_count)
    cumul = jnp.cumsum(to_blocks(-decay, block_count), axis=-1)
    carried = (doc_blocks == first_docs[:, None]).astype(jnp.float32)
    start_decay = jnp.exp(cumul) * carried[:, None, :]
    log_gap = cumul[..., :, None] - cumul[..., None, :]
    within = jnp.arange(GROUP, dtype=jnp.int32)
    same_doc = (doc_blocks[:, :, None] == doc_blocks[:, None, :]) & (
        within[:, None] >= within[None, :]
    )[None]
    pair_decay = jnp.where(same_doc[:, None], jnp.exp(jnp.minimum(log_gap, 0.0)), 0.0)
    strict = within[:, None] > within[None, :]
    key_gram = jnp.einsum("nhtd,nhsd->nhts", k, k, precision=exact_mode)
    tri_matrix = jnp.eye(GROUP, dtype=jnp.float32) + beta[..., None] * jnp.where(
        strict, pair_decay * key_gram, 0.0
    )
    solve_rhs = jnp.concatenate([beta[..., None] * v, (beta * start_decay)[..., None] * k], axis=-1)
    solved = jax.scipy.linalg.solve_triangular(
        tri_matrix, solve_rhs, lower=True, unit_diagonal=True
    )
    value_part = solved[..., :HEAD_DIM]
    state_part = solved[..., HEAD_DIM:]
    end_keys = k * pair_decay[..., -1, :][..., None]
    phi_group = start_decay[..., -1][..., None, None] * jnp.eye(HEAD_DIM, dtype=jnp.float32)
    phi_group = phi_group - jnp.einsum(
        "nhsd,nhse->nhde", end_keys, state_part, precision=exact_mode
    )
    bias_group = jnp.einsum("nhsd,nhse->nhde", end_keys, value_part, precision=exact_mode)
    return (q, k, start_decay, pair_decay, value_part, state_part, phi_group, bias_group)


def states_from(phi_group, bias_group, state_in):

    def states_group_step(state, pair):
        return (matmul_heads(pair[0], state) + pair[1], state)

    state_out, group_starts = lax.scan(states_group_step, state_in, (phi_group, bias_group))
    return (group_starts, state_out)


def device_map(phi_group, bias_group, identity, zero_state):

    def device_group_step(carry, pair):
        return (combine(carry, pair), None)

    composed, unused = lax.scan(device_group_step, (identity, zero_state), (phi_group, bias_group))
    return composed


def run_layer(query_f, key_f, value_f, beta_logit, decay, state_in, doc_blocks, first_docs):
    q, k, start_decay, pair_decay, value_part, state_part, phi_group, bias_group = group_terms(
        query_f, key_f, value_f, beta_logit, decay, doc_blocks, first_docs
    )
    group_starts, state_out = states_from(phi_group, bias_group, state_in)
    writes = value_part - jnp.einsum(
        "nhsd,nhde->nhse", state_part, group_starts, precision=exact_mode
    )
    query_key = jnp.einsum("nhtd,nhsd->nhts", q, k, precision=exact_mode)
    output = start_decay[..., None] * jnp.einsum(
        "nhtd,nhde->nhte", q, group_starts, precision=exact_mode
    )
    output = output + jnp.einsum(
        "nhts,nhse->nhte", pair_decay * query_key, writes, precision=exact_mode
    )
    tok_count = query_f.shape[0]
    return (jnp.swapaxes(output, 1, 2).reshape(tok_count, -1), state_out)


def shards(query, key, value, beta_logit, decay, out_grad, ratio, clip_mask, lengths):
    head_count = lax.axis_size("head")
    weight = ratio * clip_mask.astype(jnp.float32)
    weight_tile = jnp.broadcast_to(weight[:, None], (weight.shape[0], head_count))
    query_rows, key_rows, value_rows, grad_rows = (
        lax.all_to_all(query, "head", split_axis=1, concat_axis=0, tiled=True),
        lax.all_to_all(key, "head", split_axis=1, concat_axis=0, tiled=True),
        lax.all_to_all(value, "head", split_axis=1, concat_axis=0, tiled=True),
        lax.all_to_all(out_grad, "head", split_axis=1, concat_axis=0, tiled=True),
    )
    beta_rows, decay_rows, weight_rows = (
        lax.all_to_all(beta_logit, "head", split_axis=1, concat_axis=0, tiled=True),
        lax.all_to_all(decay, "head", split_axis=1, concat_axis=0, tiled=True),
        lax.all_to_all(weight_tile, "head", split_axis=1, concat_axis=0, tiled=True),
    )
    tok_count = query_rows.shape[0]
    block_count = tok_count // GROUP
    positions = lax.axis_index("dp") * tok_count + jnp.arange(tok_count, dtype=jnp.int32)
    doc_starts, doc_ids = segments(lengths, positions)
    doc_blocks = doc_ids.reshape(block_count, GROUP)
    first_docs = doc_blocks[:, 0] - doc_starts.reshape(block_count, GROUP)[:, 0].astype(jnp.int32)
    query_f = query_rows.astype(jnp.float32)
    key_f = key_rows.astype(jnp.float32)
    value_f = value_rows.astype(jnp.float32)
    value_heads = value_f.shape[1] // HEAD_DIM
    identity = jnp.broadcast_to(
        jnp.eye(HEAD_DIM, dtype=jnp.float32), (value_heads, HEAD_DIM, HEAD_DIM)
    )
    zero_state = jnp.zeros((value_heads, HEAD_DIM, HEAD_DIM), jnp.float32)
    span_steps = min(lax.axis_size("dp") // 2 + 1, lax.axis_size("dp") - 1)
    terms = group_terms(query_f, key_f, value_f, beta_rows, decay_rows, doc_blocks, first_docs)
    phi_device, bias_device = device_map(terms[6], terms[7], identity, zero_state)

    def relay_forward(index, state):
        return from_behind(matmul_heads(phi_device, state) + bias_device, "dp", 1)

    state_in = lax.fori_loop(0, span_steps, relay_forward, zero_state)

    def local_layer(a_in, b_in, c_in, d_in, e_in, f_in):
        return run_layer(a_in, b_in, c_in, d_in, e_in, f_in, doc_blocks, first_docs)

    layer_out, pullback = jax.vjp(
        local_layer, query_f, key_f, value_f, beta_rows, decay_rows, state_in
    )
    cotangent = grad_rows.astype(jnp.float32) * weight_rows
    first_pass = pullback((cotangent, zero_state))
    local_grad = first_pass[5]
    phi_flipped = jnp.swapaxes(phi_device, 1, 2)

    def relay_backward(index, grad):
        return from_behind(matmul_heads(phi_flipped, grad) + local_grad, "dp", -1)

    state_grad = lax.fori_loop(0, span_steps, relay_backward, zero_state)
    second_pass = pullback((jnp.zeros_like(layer_out[0]), state_grad))
    totals = [first_pass[index] + second_pass[index] for index in range(5)]
    query_back, key_back, value_back = (
        lax.all_to_all(
            totals[0].astype(jnp.bfloat16), "head", split_axis=0, concat_axis=1, tiled=True
        ),
        lax.all_to_all(
            totals[1].astype(jnp.bfloat16), "head", split_axis=0, concat_axis=1, tiled=True
        ),
        lax.all_to_all(
            totals[2].astype(jnp.bfloat16), "head", split_axis=0, concat_axis=1, tiled=True
        ),
    )
    beta_back, decay_back = (
        lax.all_to_all(totals[3], "head", split_axis=0, concat_axis=1, tiled=True),
        lax.all_to_all(totals[4], "head", split_axis=0, concat_axis=1, tiled=True),
    )
    return (query_back, key_back, value_back, beta_back, decay_back)


def solution(mesh):
    return jax.shard_map(
        shards,
        mesh=mesh,
        in_specs=(
            P(("dp", "head"), None),
            P(("dp", "head"), None),
            P(("dp", "head"), None),
            P(("dp", "head"), None),
            P(("dp", "head"), None),
            P(("dp", "head"), None),
            P(("dp", "head")),
            P(("dp", "head")),
            P(),
        ),
        out_specs=(
            P(("dp", "head"), None),
            P(("dp", "head"), None),
            P(("dp", "head"), None),
            P(("dp", "head"), None),
            P(("dp", "head"), None),
        ),
        check_vma=False,
    )
```

profile of v0, /device:TPU:250, one launch (start us, length us, event | category | flops | bytes accessed | tf_op | source)
XLA Modules:
  0.0 1094.6 jit_solution(14464403902708706530)
XLA Ops:
  55.1 39.3 %custom-call.11 = f32[2,4,1,64,64]{3,4,2,1,0:T(8,128)S(1)} custom-call(f32[2,4,1,64,64]{4,3,2,1,0:T(8,128)S(1)} %get-tuple-element.776), custom_call_target="InvertDiagBlocksLowerTriangular" | custom-call | tf_op jit(solution)/shard_map/jit(_solve_triangular)/vmap(vmap())/triangular_solve/custom-call.1 | solution.py:68
  111.2 414.1 %while.82 = (s32[]{:T(128)}, f32[4,128,128]{2,1,0:T(8,128)S(1)}, f32[4,128,128]{2,1,0:T(8,128)S(1)}, f32[4,128,128]{2,1,0:T(8,128)S(1)}, s32[]{:T(128)}) while((s32[]{:T(128)}, f32[4,128,128]{2,1,0:T(8,128)S(1)}, f32[4,128,128]{2,1,0:T(8,128)S(1)}, f32[4,128,128]{2,1,0:T(8,128)S(1)}, s32[]{:T(128)}) %tuple.217), condition=%wide.region_8.10_spmd, body=%wide.region_7.9_spmd.sunk | while | flops 100728832 | bytes 2097253 | solution.py:155
  569.7 443.1 %while.84 = (s32[]{:T(128)}, f32[4,128,128]{2,1,0:T(8,128)S(1)}, f32[4,128,128]{2,1,0:T(8,128)S(1)}, f32[4,128,128]{2,1,0:T(8,128)S(1)}, s32[]{:T(128)}) while((s32[]{:T(128)}, f32[4,128,128]{2,1,0:T(8,128)S(1)}, f32[4,128,128]{2,1,0:T(8,128)S(1)}, f32[4,128,128]{2,1,0:T(8,128)S(1)}, s32[]{:T(128)}) %tuple.226), condition=%wide.region_21.24_spmd, body=%wide.region_20.23_spmd.sunk | while | flops 100728832 | bytes 2097253 | solution.py:171
  572.7 11.9 %collective-permute-done.1 = f32[4,128,128]{2,1,0:T(8,128)S(1)} collective-permute-done((f32[4,128,128]{2,1,0:T(8,128)}, f32[4,128,128]{2,1,0:T(8,128)S(1)}, u32[]{:S(2)}, u32[]{:S(2)}) %collective-permute-start.1) | collective-permute-done | bytes 262176 | tf_op jit(solution)/shard_map/while/body/eval_jaxpr/ppermute | solution.py:16
  587.6 10.5 collective-permute-done.1
  601.2 9.9 collective-permute-done.1
  627.0 9.9 collective-permute-done.1
  639.8 9.9 collective-permute-done.1
  652.7 9.9 collective-permute-done.1
  665.6 9.9 collective-permute-done.1
  678.5 10.8 collective-permute-done.1
  692.4 12.0 %collective-permute-done.1 = f32[4,128,128]{2,1,0:T(8,128)S(1)} collective-permute-done((f32[4,128,128]{2,1,0:T(8,128)}, f32[4,128,128]{2,1,0:T(8,128)S(1)}, u32[]{:S(2)}, u32[]{:S(2)}) %collective-permute-start.1) | collective-permute-done | bytes 262176 | tf_op jit(solution)/shard_map/while/body/eval_jaxpr/ppermute | solution.py:16
  707.4 12.2 %collective-permute-done.1 = f32[4,128,128]{2,1,0:T(8,128)S(1)} collective-permute-done((f32[4,128,128]{2,1,0:T(8,128)}, f32[4,128,128]{2,1,0:T(8,128)S(1)}, u32[]{:S(2)}, u32[]{:S(2)}) %collective-permute-start.1) | collective-permute-done | bytes 262176 | tf_op jit(solution)/shard_map/while/body/eval_jaxpr/ppermute | solution.py:16
  722.6 11.4 %collective-permute-done.1 = f32[4,128,128]{2,1,0:T(8,128)S(1)} collective-permute-done((f32[4,128,128]{2,1,0:T(8,128)}, f32[4,128,128]{2,1,0:T(8,128)S(1)}, u32[]{:S(2)}, u32[]{:S(2)}) %collective-permute-start.1) | collective-permute-done | bytes 262176 | tf_op jit(solution)/shard_map/while/body/eval_jaxpr/ppermute | solution.py:16
  737.0 10.5 collective-permute-done.1
  750.5 9.9 collective-permute-done.1
  763.4 9.9 collective-permute-done.1
  776.3 9.9 collective-permute-done.1
  789.2 9.9 collective-permute-done.1
  827.8 10.9 collective-permute-done.1
  841.7 12.1 %collective-permute-done.1 = f32[4,128,128]{2,1,0:T(8,128)S(1)} collective-permute-done((f32[4,128,128]{2,1,0:T(8,128)}, f32[4,128,128]{2,1,0:T(8,128)S(1)}, u32[]{:S(2)}, u32[]{:S(2)}) %collective-permute-start.1) | collective-permute-done | bytes 262176 | tf_op jit(solution)/shard_map/while/body/eval_jaxpr/ppermute | solution.py:16
  856.8 12.1 %collective-permute-done.1 = f32[4,128,128]{2,1,0:T(8,128)S(1)} collective-permute-done((f32[4,128,128]{2,1,0:T(8,128)}, f32[4,128,128]{2,1,0:T(8,128)S(1)}, u32[]{:S(2)}, u32[]{:S(2)}) %collective-permute-start.1) | collective-permute-done | bytes 262176 | tf_op jit(solution)/shard_map/while/body/eval_jaxpr/ppermute | solution.py:16
  872.0 11.4 %collective-permute-done.1 = f32[4,128,128]{2,1,0:T(8,128)S(1)} collective-permute-done((f32[4,128,128]{2,1,0:T(8,128)}, f32[4,128,128]{2,1,0:T(8,128)S(1)}, u32[]{:S(2)}, u32[]{:S(2)}) %collective-permute-start.1) | collective-permute-done | bytes 262176 | tf_op jit(solution)/shard_map/while/body/eval_jaxpr/ppermute | solution.py:16
  886.3 10.5 collective-permute-done.1
  (586 shorter events, 843.4 us)
Async XLA Ops:
  48.0 47.1 %all-to-all-start.5 = ((bf16[16,8,512]{2,0,1:T(8,128)(2,1)}), bf16[16,8,512]{2,0,1:T(8,128)(2,1)S(1)}, u32[]{:S(2)}, u32[]{:S(2)}) async-start(bf16[16,8,512]{2,0,1:T(8,128)(2,1)} %bitcast.243), calls=%async_computation.5 | async-start | bytes 262144 | tf_op jit(solution)/shard_map/all_to_all | solution.py:126
  194.6 12.4 %collective-permute-start = (f32[4,128,128]{2,1,0:T(8,128)S(1)}, f32[4,128,128]{2,1,0:T(8,128)S(1)}, u32[]{:S(2)}, u32[]{:S(2)}) collective-permute-start(f32[4,128,128]{2,1,0:T(8,128)S(1)} %convolution_add_fusion.28), channel_id=1, source_target_pairs={{0,8},{8,16},{16,24},{24,32},{32,40},{40,48},{48,56},{56,64},{64,7... | collective-permute-start | bytes 786440 | tf_op jit(solution)/shard_map/while/body/eval_jaxpr/ppermute | solution.py:16
  207.4 13.6 %collective-permute-start = (f32[4,128,128]{2,1,0:T(8,128)S(1)}, f32[4,128,128]{2,1,0:T(8,128)S(1)}, u32[]{:S(2)}, u32[]{:S(2)}) collective-permute-start(f32[4,128,128]{2,1,0:T(8,128)S(1)} %convolution_add_fusion.28), channel_id=1, source_target_pairs={{0,8},{8,16},{16,24},{24,32},{32,40},{40,48},{48,56},{56,64},{64,7... | collective-permute-start | bytes 786440 | tf_op jit(solution)/shard_map/while/body/eval_jaxpr/ppermute | solution.py:16
  221.3 14.1 %collective-permute-start = (f32[4,128,128]{2,1,0:T(8,128)S(1)}, f32[4,128,128]{2,1,0:T(8,128)S(1)}, u32[]{:S(2)}, u32[]{:S(2)}) collective-permute-start(f32[4,128,128]{2,1,0:T(8,128)S(1)} %convolution_add_fusion.28), channel_id=1, source_target_pairs={{0,8},{8,16},{16,24},{24,32},{32,40},{40,48},{48,56},{56,64},{64,7... | collective-permute-start | bytes 786440 | tf_op jit(solution)/shard_map/while/body/eval_jaxpr/ppermute | solution.py:16
  235.8 13.2 %collective-permute-start = (f32[4,128,128]{2,1,0:T(8,128)S(1)}, f32[4,128,128]{2,1,0:T(8,128)S(1)}, u32[]{:S(2)}, u32[]{:S(2)}) collective-permute-start(f32[4,128,128]{2,1,0:T(8,128)S(1)} %convolution_add_fusion.28), channel_id=1, source_target_pairs={{0,8},{8,16},{16,24},{24,32},{32,40},{40,48},{48,56},{56,64},{64,7... | collective-permute-start | bytes 786440 | tf_op jit(solution)/shard_map/while/body/eval_jaxpr/ppermute | solution.py:16
  249.4 12.4 %collective-permute-start = (f32[4,128,128]{2,1,0:T(8,128)S(1)}, f32[4,128,128]{2,1,0:T(8,128)S(1)}, u32[]{:S(2)}, u32[]{:S(2)}) collective-permute-start(f32[4,128,128]{2,1,0:T(8,128)S(1)} %convolution_add_fusion.28), channel_id=1, source_target_pairs={{0,8},{8,16},{16,24},{24,32},{32,40},{40,48},{48,56},{56,64},{64,7... | collective-permute-start | bytes 786440 | tf_op jit(solution)/shard_map/while/body/eval_jaxpr/ppermute | solution.py:16
  334.7 13.3 %collective-permute-start = (f32[4,128,128]{2,1,0:T(8,128)S(1)}, f32[4,128,128]{2,1,0:T(8,128)S(1)}, u32[]{:S(2)}, u32[]{:S(2)}) collective-permute-start(f32[4,128,128]{2,1,0:T(8,128)S(1)} %convolution_add_fusion.28), channel_id=1, source_target_pairs={{0,8},{8,16},{16,24},{24,32},{32,40},{40,48},{48,56},{56,64},{64,7... | collective-permute-start | bytes 786440 | tf_op jit(solution)/shard_map/while/body/eval_jaxpr/ppermute | solution.py:16
  348.4 14.3 %collective-permute-start = (f32[4,128,128]{2,1,0:T(8,128)S(1)}, f32[4,128,128]{2,1,0:T(8,128)S(1)}, u32[]{:S(2)}, u32[]{:S(2)}) collective-permute-start(f32[4,128,128]{2,1,0:T(8,128)S(1)} %convolution_add_fusion.28), channel_id=1, source_target_pairs={{0,8},{8,16},{16,24},{24,32},{32,40},{40,48},{48,56},{56,64},{64,7... | collective-permute-start | bytes 786440 | tf_op jit(solution)/shard_map/while/body/eval_jaxpr/ppermute | solution.py:16
  363.2 13.4 %collective-permute-start = (f32[4,128,128]{2,1,0:T(8,128)S(1)}, f32[4,128,128]{2,1,0:T(8,128)S(1)}, u32[]{:S(2)}, u32[]{:S(2)}) collective-permute-start(f32[4,128,128]{2,1,0:T(8,128)S(1)} %convolution_add_fusion.28), channel_id=1, source_target_pairs={{0,8},{8,16},{16,24},{24,32},{32,40},{40,48},{48,56},{56,64},{64,7... | collective-permute-start | bytes 786440 | tf_op jit(solution)/shard_map/while/body/eval_jaxpr/ppermute | solution.py:16
  377.0 12.6 %collective-permute-start = (f32[4,128,128]{2,1,0:T(8,128)S(1)}, f32[4,128,128]{2,1,0:T(8,128)S(1)}, u32[]{:S(2)}, u32[]{:S(2)}) collective-permute-start(f32[4,128,128]{2,1,0:T(8,128)S(1)} %convolution_add_fusion.28), channel_id=1, source_target_pairs={{0,8},{8,16},{16,24},{24,32},{32,40},{40,48},{48,56},{56,64},{64,7... | collective-permute-start | bytes 786440 | tf_op jit(solution)/shard_map/while/body/eval_jaxpr/ppermute | solution.py:16
  462.1 12.8 %collective-permute-start = (f32[4,128,128]{2,1,0:T(8,128)S(1)}, f32[4,128,128]{2,1,0:T(8,128)S(1)}, u32[]{:S(2)}, u32[]{:S(2)}) collective-permute-start(f32[4,128,128]{2,1,0:T(8,128)S(1)} %convolution_add_fusion.28), channel_id=1, source_target_pairs={{0,8},{8,16},{16,24},{24,32},{32,40},{40,48},{48,56},{56,64},{64,7... | collective-permute-start | bytes 786440 | tf_op jit(solution)/shard_map/while/body/eval_jaxpr/ppermute | solution.py:16
  475.4 14.0 %collective-permute-start = (f32[4,128,128]{2,1,0:T(8,128)S(1)}, f32[4,128,128]{2,1,0:T(8,128)S(1)}, u32[]{:S(2)}, u32[]{:S(2)}) collective-permute-start(f32[4,128,128]{2,1,0:T(8,128)S(1)} %convolution_add_fusion.28), channel_id=1, source_target_pairs={{0,8},{8,16},{16,24},{24,32},{32,40},{40,48},{48,56},{56,64},{64,7... | collective-permute-start | bytes 786440 | tf_op jit(solution)/shard_map/while/body/eval_jaxpr/ppermute | solution.py:16
  570.8 13.8 %collective-permute-start.1 = (f32[4,128,128]{2,1,0:T(8,128)}, f32[4,128,128]{2,1,0:T(8,128)S(1)}, u32[]{:S(2)}, u32[]{:S(2)}) collective-permute-start(f32[4,128,128]{2,1,0:T(8,128)} %convolution_add_fusion.30), channel_id=1, source_target_pairs={{8,0},{16,8},{24,16},{32,24},{40,32},{48,40},{56,48},{64,56},{72,6... | collective-permute-start | bytes 786440 | tf_op jit(solution)/shard_map/while/body/eval_jaxpr/ppermute | solution.py:16
  585.7 12.4 %collective-permute-start.1 = (f32[4,128,128]{2,1,0:T(8,128)}, f32[4,128,128]{2,1,0:T(8,128)S(1)}, u32[]{:S(2)}, u32[]{:S(2)}) collective-permute-start(f32[4,128,128]{2,1,0:T(8,128)} %convolution_add_fusion.30), channel_id=1, source_target_pairs={{8,0},{16,8},{24,16},{32,24},{40,32},{48,40},{56,48},{64,56},{72,6... | collective-permute-start | bytes 786440 | tf_op jit(solution)/shard_map/while/body/eval_jaxpr/ppermute | solution.py:16
  676.6 12.8 %collective-permute-start.1 = (f32[4,128,128]{2,1,0:T(8,128)}, f32[4,128,128]{2,1,0:T(8,128)S(1)}, u32[]{:S(2)}, u32[]{:S(2)}) collective-permute-start(f32[4,128,128]{2,1,0:T(8,128)} %convolution_add_fusion.30), channel_id=1, source_target_pairs={{8,0},{16,8},{24,16},{32,24},{40,32},{48,40},{56,48},{64,56},{72,6... | collective-permute-start | bytes 786440 | tf_op jit(solution)/shard_map/while/body/eval_jaxpr/ppermute | solution.py:16
  690.4 13.9 %collective-permute-start.1 = (f32[4,128,128]{2,1,0:T(8,128)}, f32[4,128,128]{2,1,0:T(8,128)S(1)}, u32[]{:S(2)}, u32[]{:S(2)}) collective-permute-start(f32[4,128,128]{2,1,0:T(8,128)} %convolution_add_fusion.30), channel_id=1, source_target_pairs={{8,0},{16,8},{24,16},{32,24},{40,32},{48,40},{56,48},{64,56},{72,6... | collective-permute-start | bytes 786440 | tf_op jit(solution)/shard_map/while/body/eval_jaxpr/ppermute | solution.py:16
  705.5 14.1 %collective-permute-start.1 = (f32[4,128,128]{2,1,0:T(8,128)}, f32[4,128,128]{2,1,0:T(8,128)S(1)}, u32[]{:S(2)}, u32[]{:S(2)}) collective-permute-start(f32[4,128,128]{2,1,0:T(8,128)} %convolution_add_fusion.30), channel_id=1, source_target_pairs={{8,0},{16,8},{24,16},{32,24},{40,32},{48,40},{56,48},{64,56},{72,6... | collective-permute-start | bytes 786440 | tf_op jit(solution)/shard_map/while/body/eval_jaxpr/ppermute | solution.py:16
  720.7 13.3 %collective-permute-start.1 = (f32[4,128,128]{2,1,0:T(8,128)}, f32[4,128,128]{2,1,0:T(8,128)S(1)}, u32[]{:S(2)}, u32[]{:S(2)}) collective-permute-start(f32[4,128,128]{2,1,0:T(8,128)} %convolution_add_fusion.30), channel_id=1, source_target_pairs={{8,0},{16,8},{24,16},{32,24},{40,32},{48,40},{56,48},{64,56},{72,6... | collective-permute-start | bytes 786440 | tf_op jit(solution)/shard_map/while/body/eval_jaxpr/ppermute | solution.py:16
  735.1 12.4 %collective-permute-start.1 = (f32[4,128,128]{2,1,0:T(8,128)}, f32[4,128,128]{2,1,0:T(8,128)S(1)}, u32[]{:S(2)}, u32[]{:S(2)}) collective-permute-start(f32[4,128,128]{2,1,0:T(8,128)} %convolution_add_fusion.30), channel_id=1, source_target_pairs={{8,0},{16,8},{24,16},{32,24},{40,32},{48,40},{56,48},{64,56},{72,6... | collective-permute-start | bytes 786440 | tf_op jit(solution)/shard_map/while/body/eval_jaxpr/ppermute | solution.py:16
  825.9 12.8 %collective-permute-start.1 = (f32[4,128,128]{2,1,0:T(8,128)}, f32[4,128,128]{2,1,0:T(8,128)S(1)}, u32[]{:S(2)}, u32[]{:S(2)}) collective-permute-start(f32[4,128,128]{2,1,0:T(8,128)} %convolution_add_fusion.30), channel_id=1, source_target_pairs={{8,0},{16,8},{24,16},{32,24},{40,32},{48,40},{56,48},{64,56},{72,6... | collective-permute-start | bytes 786440 | tf_op jit(solution)/shard_map/while/body/eval_jaxpr/ppermute | solution.py:16
  839.8 14.0 %collective-permute-start.1 = (f32[4,128,128]{2,1,0:T(8,128)}, f32[4,128,128]{2,1,0:T(8,128)S(1)}, u32[]{:S(2)}, u32[]{:S(2)}) collective-permute-start(f32[4,128,128]{2,1,0:T(8,128)} %convolution_add_fusion.30), channel_id=1, source_target_pairs={{8,0},{16,8},{24,16},{32,24},{40,32},{48,40},{56,48},{64,56},{72,6... | collective-permute-start | bytes 786440 | tf_op jit(solution)/shard_map/while/body/eval_jaxpr/ppermute | solution.py:16
  854.9 14.1 %collective-permute-start.1 = (f32[4,128,128]{2,1,0:T(8,128)}, f32[4,128,128]{2,1,0:T(8,128)S(1)}, u32[]{:S(2)}, u32[]{:S(2)}) collective-permute-start(f32[4,128,128]{2,1,0:T(8,128)} %convolution_add_fusion.30), channel_id=1, source_target_pairs={{8,0},{16,8},{24,16},{32,24},{40,32},{48,40},{56,48},{64,56},{72,6... | collective-permute-start | bytes 786440 | tf_op jit(solution)/shard_map/while/body/eval_jaxpr/ppermute | solution.py:16
  870.0 13.3 %collective-permute-start.1 = (f32[4,128,128]{2,1,0:T(8,128)}, f32[4,128,128]{2,1,0:T(8,128)S(1)}, u32[]{:S(2)}, u32[]{:S(2)}) collective-permute-start(f32[4,128,128]{2,1,0:T(8,128)} %convolution_add_fusion.30), channel_id=1, source_target_pairs={{8,0},{16,8},{24,16},{32,24},{40,32},{48,40},{56,48},{64,56},{72,6... | collective-permute-start | bytes 786440 | tf_op jit(solution)/shard_map/while/body/eval_jaxpr/ppermute | solution.py:16
  884.4 12.4 %collective-permute-start.1 = (f32[4,128,128]{2,1,0:T(8,128)}, f32[4,128,128]{2,1,0:T(8,128)S(1)}, u32[]{:S(2)}, u32[]{:S(2)}) collective-permute-start(f32[4,128,128]{2,1,0:T(8,128)} %convolution_add_fusion.30), channel_id=1, source_target_pairs={{8,0},{16,8},{24,16},{32,24},{40,32},{48,40},{56,48},{64,56},{72,6... | collective-permute-start | bytes 786440 | tf_op jit(solution)/shard_map/while/body/eval_jaxpr/ppermute | solution.py:16
  (142 other events, 812.9 us)
where the time goes:
time: 1110 us; the launch traced here: 1090 us
  waiting for transfers between devices  521 us (47%)
  starting transfers between devices  372 us (34%)
  matrix products  103 us (9%)
  other arithmetic  51.4 us (5%)
  local copies, waits for them, and re-layouts  42.8 us (4%)
    ppermute x66, waiting for transfers between devices, from_behind(): return lax.ppermute(block, axis, route)  493 us
    ppermute x66, starting transfers between devices, from_behind(): return lax.ppermute(block, axis, route)  314 us
    dot_general x80, matrix products, matmul_heads(): return jnp.einsum('hij,hjk->hik', left, right, precision=exact_mode)  55.8 us
    another operation x4, other arithmetic, group_terms(): jax.scipy.linalg.solve_triangular(tri_matrix, solve_rhs, lower=True, unit...  39.4 us
  transfers between devices with their start and end apart: 78, of which 75 were waited for; matrix products, arithmetic and copies ran while one was open for 5% of the time, Pallas kernels for 0%

commit v1 on v0

v1 whole, which is shorter than its diff:
```python
import functools

import jax
import jax.numpy as jnp
from jax import lax
from jax.experimental import pallas as pl
from jax.experimental.pallas import tpu as pltpu
from jax.sharding import PartitionSpec as P

HEAD_DIM = 128
TILE = 128
HEADS = 32
ROWS = 16
SPAN = HEADS * ROWS
TILES = SPAN // TILE
HOPS = 8
NDOCS = 16
SCALE = HEAD_DIM ** (-0.5)
MESH = pl.DeviceIdType.MESH
F32 = jnp.float32
BF16 = jnp.bfloat16
LIMIT = 56 * 1024 * 1024


def product(left, right, over=(1, 0)):
    return lax.dot_general(
        left, right, (((over[0],), (over[1],)), ((), ())), preferred_element_type=F32
    )


def halves(values):
    high = values.astype(BF16)
    return high, (values - high.astype(F32)).astype(BF16)


def thirds(values):
    high, rest = values.astype(BF16), None
    rest = values - high.astype(F32)
    middle = rest.astype(BF16)
    return high, middle, (rest - middle.astype(F32)).astype(BF16)


def product3(left, right, over=(1, 0)):
    (lh, ll), (rh, rl) = left, right
    return product(lh, rh, over) + (product(lh, rl, over) + product(ll, rh, over))


def product2l(left, right, over=(1, 0)):
    return product(left[0], right, over) + product(left[1], right, over)


def product2r(left, right, over=(1, 0)):
    return product(left, right[0], over) + product(left, right[1], over)


def iota(shape, axis):
    return lax.broadcasted_iota(jnp.int32, shape, axis)


def band(index):
    return slice(index * TILE, (index + 1) * TILE)


def place():
    dp, head = lax.axis_index("dp"), lax.axis_index("head")
    base = lax.div(dp, 4) * 4
    me = lax.rem(dp, 4) * 8 + head

    def device(index):
        return (base + lax.div(index, 8), lax.rem(index, 8))

    return dp, head, me, device


def greet_plane(me, device):
    barrier = pltpu.get_barrier_semaphore()

    def greet(offset, carry):
        target = lax.rem(me + offset, HEADS)
        pl.semaphore_signal(barrier, inc=1, device_id=device(target), device_id_type=MESH)
        return carry

    lax.fori_loop(1, HEADS, greet, 0)
    return barrier


def trade_plane(me, device, sent, landed, send_sem, recv_sem):
    def send(offset, carry):
        target = lax.rem(me + offset, HEADS)
        pltpu.make_async_remote_copy(
            src_ref=sent.at[target],
            dst_ref=landed.at[me],
            send_sem=send_sem,
            recv_sem=recv_sem,
            device_id=device(target),
            device_id_type=MESH,
        ).start()
        return carry

    lax.fori_loop(1, HEADS, send, 0)
    landed[me] = sent[me]
    others = pl.ds(0, HEADS - 1)
    pltpu.make_async_copy(sent.at[others], landed.at[others], recv_sem).wait()
    pltpu.make_async_copy(sent.at[others], landed.at[others], send_sem).wait()


def exchange_in(q_ref, k_ref, v_ref, g_ref, w_ref, out_ref, sent, landed, send_sem, recv_sem):
    _, _, me, device = place()
    barrier = greet_plane(me, device)
    parts = [p.astype(F32) for p in thirds(w_ref[...])]
    lane = iota((ROWS, TILE), 1) % 32
    for j in range(HEADS):
        pair = slice((j // 2) * HEAD_DIM, (j // 2 + 1) * HEAD_DIM)
        own = slice(j * HEAD_DIM, (j + 1) * HEAD_DIM)
        sent[j, 0:16, :] = q_ref[:, pair]
        sent[j, 16:32, :] = k_ref[:, pair]
        sent[j, 32:48, :] = v_ref[:, own]
        sent[j, 48:64, :] = g_ref[:, own]
        small = jnp.zeros((ROWS, TILE), F32)
        for n in range(3):
            moved = pltpu.roll(parts[n], (TILE - j + n) % TILE, 1)
            small = jnp.where(lane == n, moved, small)
        sent[j, 64:80, :] = small.astype(BF16)
    pl.semaphore_wait(barrier, HEADS - 1)
    trade_plane(me, device, sent, landed, send_sem, recv_sem)
    out_ref[...] = landed[...]


def raw_parts(in_ref):
    return [in_ref[:, n * 16 : n * 16 + 16, :].reshape(SPAN, TILE) for n in range(5)]


def local_first(
    lengths_ref, in_ref,
    phi_ref, phit_ref, bt_ref, lt_ref, u0_ref, wk_ref, x0_ref, xk_ref, gqk_ref, gkk_ref,
    vec_ref, a_ref, pw_ref, th_ref, tl_ref,
):
    base = lax.div(lax.axis_index("dp"), 4) * SPAN
    qr, kr, vr, gr, small = raw_parts(in_ref)
    qf, kf = qr.astype(F32), kr.astype(F32)
    pick_row, pick_col = iota((TILE, 3 * TILE), 0), iota((TILE, 3 * TILE), 1)
    pick = (pick_row // 32 == pick_col // TILE) & (pick_row % 32 < 3)
    spread = product(small, pick.astype(F32).astype(BF16))
    beta = jax.nn.sigmoid(spread[:, 0:TILE])
    weight = spread[:, 2 * TILE :]
    sk = lax.rsqrt(jnp.sum(kf * kf, axis=1, keepdims=True) + 1e-06)
    sk = jnp.broadcast_to(sk, (SPAN, TILE))
    csw = lax.rsqrt(jnp.sum(qf * qf, axis=1, keepdims=True) + 1e-06) * SCALE * weight
    lower = (iota((SPAN, SPAN), 0) >= iota((SPAN, SPAN), 1)).astype(F32).astype(BF16)
    running = product(lower, small)
    lane = iota((SPAN, TILE), 1)
    running = jnp.where(lane // 32 == 1, running, 0.0)
    cumul = -jnp.broadcast_to(jnp.sum(running, axis=1, keepdims=True), (SPAN, TILE))
    start = jnp.full((SPAN, TILE), -base, jnp.int32)
    last_start = -base
    row = iota((SPAN, TILE), 0)
    bound = -base
    for n in range(NDOCS - 1):
        bound = bound + lengths_ref[n]
        start = jnp.where(row >= bound, bound, start)
        last_start = jnp.where(bound <= SPAN - 1, bound, last_start)
    gamma = jnp.where(start < 0, jnp.exp(cumul), 0.0)
    last = cumul[SPAN - 1 : SPAN, :]
    end = jnp.where(row >= last_start, jnp.exp(jnp.minimum(last - cumul, 0.0)), 0.0)
    vec_ref[0] = beta
    vec_ref[1] = gamma
    vec_ref[2] = csw
    vec_ref[3] = sk
    vec_ref[4] = end
    pack = jnp.where(lane == 0, cumul, jnp.where(lane == 1, sk, 0.0))
    across = jnp.transpose(pack)
    tok, src = iota((TILE, TILE), 0), iota((TILE, TILE), 1)
    for i in range(TILES):
        bi = band(i)
        for j in range(i + 1):
            bj = band(j)
            gap = cumul[bi] - across[0:1, bj]
            seen = src + j * TILE >= start[bi]
            if i == j:
                seen = seen & (tok >= src)
            pair = jnp.where(seen, jnp.exp(jnp.minimum(gap, 0.0)), 0.0) * across[1:2, bj]
            gqk = pair * csw[bi]
            gkk = pair * (beta[bi] * sk[bi])
            if i == j:
                gkk = jnp.where(tok > src, gkk, 0.0)
            gqk_ref[bi, bj] = gqk
            gkk_ref[bi, bj] = gkk
            a_ref[bi, bj] = gkk * product(kr[bi], kr[bj], (1, 1))
            pw_ref[bi, bj] = gqk * product(qr[bi], kr[bj], (1, 1))
    eye = (tok == src).astype(F32)
    inverse = [eye - jnp.where(tok // 2 == src // 2, a_ref[band(i), band(i)], 0.0) for i in range(TILES)]
    size = 2
    while size < TILE:
        inside = (tok // (2 * size) == src // (2 * size)) & (tok // size != src // size)
        for i in range(TILES):
            block = halves(jnp.where(inside, a_ref[band(i), band(i)], 0.0))
            parts = halves(inverse[i])
            inverse[i] = inverse[i] - product3(parts, halves(product3(block, parts)))
        size *= 2
    for i in range(TILES):
        th_ref[band(i), band(i)], tl_ref[band(i), band(i)] = halves(inverse[i])
    size = TILE
    while size < SPAN:
        for n in range(SPAN // (2 * size)):
            top = slice(2 * n * size, (2 * n + 1) * size)
            low = slice((2 * n + 1) * size, (2 * n + 2) * size)
            right = product3(halves(a_ref[low, top]), (th_ref[top, top], tl_ref[top, top]))
            block = -product3((th_ref[low, low], tl_ref[low, low]), halves(right))
            th_ref[low, top], tl_ref[low, top] = halves(block)
            th_ref[top, low] = jnp.zeros((size, size), BF16)
            tl_ref[top, low] = jnp.zeros((size, size), BF16)
        size *= 2
    keys = sk * kf
    rhs = halves(jnp.concatenate([beta * vr.astype(F32), beta * gamma * keys], axis=1))
    solved = []
    for i in range(TILES):
        bi, upto = band(i), slice(0, (i + 1) * TILE)
        part = product3((th_ref[bi, upto], tl_ref[bi, upto]), (rhs[0][upto], rhs[1][upto]))
        u0_ref[bi] = part[:, :TILE]
        wk_ref[bi] = part[:, TILE:]
        solved.append(part)
    solved = halves(jnp.concatenate(solved, axis=0))
    end_keys = end * keys
    ends = halves(end_keys)
    both = product3(solved, ends, (0, 0))
    bt_ref[...] = both[:TILE]
    phit = gamma[SPAN - 1 : SPAN, :] * eye - both[TILE:]
    phit_ref[...] = phit
    phi_ref[...] = jnp.transpose(phit)
    wks = (solved[0][:, TILE:], solved[1][:, TILE:])
    reads = []
    for i in range(TILES):
        bi, upto = band(i), slice(0, (i + 1) * TILE)
        part = product3(halves(pw_ref[bi, upto]), (wks[0][upto], wks[1][upto]))
        reads.append(gamma[bi] * csw[bi] * qf[bi] - part)
    lt_ref[...] = product2r(gr, halves(jnp.concatenate(reads, axis=0)), (0, 0))
    pulled = []
    for j in range(TILES):
        bj, onward = band(j), slice(j * TILE, SPAN)
        pulled.append(product2l(halves(pw_ref[onward, bj]), gr[onward], (0, 0)))
    pulled = halves(jnp.concatenate([jnp.concatenate(pulled, axis=0), end_keys], axis=1))
    for j in range(TILES):
        bj, onward = band(j), slice(j * TILE, SPAN)
        part = product3(
            (th_ref[onward, bj], tl_ref[onward, bj]), (pulled[0][onward], pulled[1][onward]), (0, 0)
        )
        x0_ref[bj] = part[:, :TILE]
        xk_ref[bj] = part[:, TILE:]


def relay(
    phi_ref, phit_ref, bt_ref, lt_ref, state_ref, grad_ref,
    state_in, grad_in, state_out, grad_out, send_sems, recv_sems,
):
    dp, head = lax.axis_index("dp"), lax.axis_index("head")
    count = lax.axis_size("dp")
    after = (lax.rem(dp + 4, count), head)
    before = (lax.rem(dp + count - 4, count), head)
    barrier = pltpu.get_barrier_semaphore()
    for neighbour in (after, before):
        pl.semaphore_signal(barrier, inc=1, device_id=neighbour, device_id_type=MESH)
    pl.semaphore_wait(barrier, 2)
    phi, phit = halves(phi_ref[...]), halves(phit_ref[...])

    def copy(way, step):
        source, target = ((state_out, state_in), (grad_out, grad_in))[way]
        return pltpu.make_async_remote_copy(
            src_ref=source.at[step],
            dst_ref=target.at[step],
            send_sem=send_sems.at[way, step],
            recv_sem=recv_sems.at[way, step],
            device_id=(after, before)[way],
            device_id_type=MESH,
        )

    copies = []
    for step in range(HOPS):
        for way in range(2):
            local = (bt_ref, lt_ref)[way]
            if step == 0:
                value = local[...]
            else:
                copies[-2].wait_recv()
                arrived = (state_in, grad_in)[way][step - 1]
                value = product3(halves(arrived), (phit, phi)[way]) + local[...]
            (state_out, grad_out)[way][step] = value
            copies.append(copy(way, step))
            copies[-1].start()
    copies[-2].wait_recv()
    copies[-1].wait_recv()
    state_ref[...] = state_in[HOPS - 1]
    grad_ref[...] = grad_in[HOPS - 1]
    for one in copies:
        one.wait_send()


def local_second(
    in_ref, state_ref, grad_ref, phit_ref, bt_ref, u0_ref, wk_ref, x0_ref, xk_ref, gqk_ref, gkk_ref,
    vec_ref, dirs_ref, dv_ref, small_ref, fqh_ref, fql_ref, fkh_ref, fkl_ref,
):
    _, _, me, _ = place()
    qr, kr, vr, gr, _ = raw_parts(in_ref)
    beta, gamma, csw, sk, end = [vec_ref[n] for n in range(5)]
    state, grad = halves(state_ref[...]), halves(grad_ref[...])
    u = u0_ref[...] - product3(halves(wk_ref[...]), state, (1, 1))
    x = x0_ref[...] + product3(halves(xk_ref[...]), grad, (1, 1))
    dv = beta * x
    dv_ref[...] = dv.astype(BF16)
    (uh, ul), (xh, xl) = halves(u), halves(x)
    for i in range(TILES):
        bi = band(i)
        for j in range(i + 1):
            bj = band(j)
            read = product2r(gr[bi], (uh[bj], ul[bj]), (1, 1))
            solve = product3((xh[bi], xl[bi]), (uh[bj], ul[bj]), (1, 1))
            fqh_ref[bi, bj], fql_ref[bi, bj] = halves(gqk_ref[bi, bj] * read)
            fkh_ref[bi, bj], fkl_ref[bi, bj] = halves(-gkk_ref[bi, bj] * solve)
    dq = csw * gamma * product2r(gr, state)
    dk = end * sk * product3((uh, ul), grad) - beta * gamma * sk * product3((xh, xl), state)
    dqs, dks = [], []
    for i in range(TILES):
        bi, upto, onward = band(i), slice(0, (i + 1) * TILE), slice(i * TILE, SPAN)
        dqs.append(dq[bi] + product2l((fqh_ref[bi, upto], fql_ref[bi, upto]), kr[upto]))
        part = product2l((fqh_ref[onward, bi], fql_ref[onward, bi]), qr[onward], (0, 0))
        part = part + product2l((fkh_ref[onward, bi], fkl_ref[onward, bi]), kr[onward], (0, 0))
        part = part + product2l((fkh_ref[bi, upto], fkl_ref[bi, upto]), kr[upto])
        dks.append(dk[bi] + part)
    dq, dk = jnp.concatenate(dqs, axis=0), jnp.concatenate(dks, axis=0)
    dirs_ref[0] = dq
    dirs_ref[1] = dk
    after = product3(state, halves(phit_ref[...])) + bt_ref[...]
    total = jnp.sum(jnp.sum(grad_ref[...] * after, axis=1, keepdims=True), axis=0, keepdims=True)
    xu = jnp.sum(x * u, axis=1, keepdims=True)
    cumul = jnp.sum(
        qr.astype(F32) * dq - kr.astype(F32) * dk - 2.0 * (vr.astype(F32) * dv), axis=1, keepdims=True
    )
    cumul = cumul + 2.0 * xu
    cumul = jnp.where(iota((SPAN, 1), 0) == SPAN - 1, cumul + total, cumul)
    lane = iota((SPAN, TILE), 1)
    cumul = jnp.broadcast_to(cumul, (SPAN, TILE))
    pieces = [p.astype(F32) for p in thirds(cumul)]
    packed = jnp.zeros((SPAN, TILE), F32)
    for n in range(3):
        packed = jnp.where(lane == n, pieces[n], packed)
    upper = (iota((SPAN, SPAN), 0) <= iota((SPAN, SPAN), 1)).astype(F32).astype(BF16)
    ddecay = -jnp.sum(product(upper, packed.astype(BF16)), axis=1, keepdims=True)
    dbeta = xu * (1.0 - beta)
    ddecay = jnp.broadcast_to(ddecay, (SPAN, TILE))
    out = jnp.zeros((SPAN, TILE), F32)
    for n, values in enumerate((dbeta, ddecay)):
        high, low = halves(values)
        out = jnp.where(lane == me + 32 * n, high.astype(F32), out)
        out = jnp.where(lane == me + 32 * n + 64, low.astype(F32), out)
    small_ref[...] = out.astype(BF16)


def exchange_out(
    in_ref, dirs_ref, dv_ref, small_ref, dq_ref, dk_ref, dvo_ref, db_ref, dd_ref,
    partner_in, sent, landed, send_sem, recv_sem, pair_send, pair_recv,
):
    dp, head, me, device = place()
    core = lax.rem(head, 2)
    barrier = greet_plane(me, device)
    pl.semaphore_wait(barrier, HEADS - 1)
    pair = pltpu.make_async_remote_copy(
        src_ref=dirs_ref.at[1 - core],
        dst_ref=partner_in,
        send_sem=pair_send,
        recv_sem=pair_recv,
        device_id=(dp, head + 1 - 2 * core),
        device_id_type=MESH,
    )
    pair.start()
    own = jnp.where(core == 0, in_ref[:, 0:16, :], in_ref[:, 16:32, :]).reshape(SPAN, TILE)
    own = own.astype(F32)
    inverse = 1.0 / (jnp.sum(own * own, axis=1, keepdims=True) + 1e-06)
    sent[:, 16:32, :] = dv_ref[...].reshape(HEADS, ROWS, TILE)
    sent[:, 32:48, :] = small_ref[...].reshape(HEADS, ROWS, TILE)
    pair.wait_recv()
    grad = dirs_ref[core] + partner_in[...]
    grad = grad - own * (jnp.sum(own * grad, axis=1, keepdims=True) * inverse)
    sent[:, 0:16, :] = grad.astype(BF16).reshape(HEADS, ROWS, TILE)
    trade_plane(me, device, sent, landed, send_sem, recv_sem)
    total = jnp.zeros((ROWS, TILE), F32)
    for j in range(HEADS):
        to_ref = (dq_ref, dk_ref)[j % 2]
        to_ref[:, (j // 2) * HEAD_DIM : (j // 2 + 1) * HEAD_DIM] = landed[j, 0:16, :]
        dvo_ref[:, j * HEAD_DIM : (j + 1) * HEAD_DIM] = landed[j, 16:32, :]
        total = total + landed[j, 32:48, :].astype(F32)
    total = total + pltpu.roll(total, 64, 1)
    db_ref[...] = total[:, 0:32]
    dd_ref[...] = total[:, 32:64]
    pair.wait_send()


def call(body, outs, scratch, collective=None, smem=False, n_in=0, flops=0, name=None):
    vmem = pl.BlockSpec(memory_space=pltpu.VMEM)
    in_specs = [vmem] * n_in
    if smem:
        in_specs = [pl.BlockSpec(memory_space=pltpu.SMEM)] + in_specs[1:]
    if collective is None:
        params = pltpu.CompilerParams(vmem_limit_bytes=LIMIT)
    else:
        params = pltpu.CompilerParams(
            vmem_limit_bytes=LIMIT, collective_id=collective, has_side_effects=True
        )
    return pl.pallas_call(
        body,
        out_shape=[jax.ShapeDtypeStruct(s, d) for s, d in outs],
        in_specs=in_specs,
        out_specs=[vmem] * len(outs),
        scratch_shapes=scratch,
        compiler_params=params,
        cost_estimate=pl.CostEstimate(flops=flops, bytes_accessed=1 << 20, transcendentals=0),
        name=name,
    )


def shards(query, key, value, beta_logit, decay, out_grad, ratio, clip_mask, lengths):
    weight = ratio * clip_mask.astype(F32)
    wide = jnp.broadcast_to(weight[:, None], (ROWS, 64))
    columns = jnp.concatenate([beta_logit, decay, wide], axis=1)
    dma = pltpu.SemaphoreType.DMA
    square, tall, big = (TILE, TILE), (SPAN, TILE), (SPAN, SPAN)
    block_in = (HEADS, 80, TILE)
    (rows,) = call(
        exchange_in,
        [(block_in, BF16)],
        [pltpu.VMEM(block_in, BF16), pltpu.VMEM(block_in, BF16), dma, dma],
        collective=0,
        n_in=5,
        name="exchange_in",
    )(query, key, value, out_grad, columns)
    first = call(
        local_first,
        [(square, F32)] * 4 + [(tall, F32)] * 4 + [(big, F32)] * 2 + [((5,) + tall, F32)],
        [pltpu.VMEM(big, F32), pltpu.VMEM(big, F32), pltpu.VMEM(big, BF16), pltpu.VMEM(big, BF16)],
        n_in=2,
        smem=True,
        name="local_first",
    )(lengths, rows)
    phi, phit, bt, lt, u0, wk, x0, xk, gqk, gkk, vec = first
    slots = pltpu.VMEM((HOPS,) + square, F32)
    state, grad = call(
        relay,
        [(square, F32)] * 2,
        [slots] * 4 + [dma((2, HOPS)), dma((2, HOPS))],
        collective=1,
        n_in=4,
        name="relay",
    )(phi, phit, bt, lt)
    dirs, dv, small = call(
        local_second,
        [((2,) + tall, F32), (tall, BF16), (tall, BF16)],
        [pltpu.VMEM(big, BF16)] * 4,
        n_in=12,
        name="local_second",
    )(rows, state, grad, phit, bt, u0, wk, x0, xk, gqk, gkk, vec)
    block_out = (HEADS, 48, TILE)
    wide_out = HEADS * HEAD_DIM
    return tuple(
        call(
            exchange_out,
            [
                ((ROWS, wide_out // 2), BF16),
                ((ROWS, wide_out // 2), BF16),
                ((ROWS, wide_out), BF16),
                ((ROWS, HEADS), F32),
                ((ROWS, HEADS), F32),
            ],
            [pltpu.VMEM(tall, F32), pltpu.VMEM(block_out, BF16), pltpu.VMEM(block_out, BF16)]
            + [dma] * 4,
            collective=2,
            n_in=4,
            name="exchange_out",
        )(rows, dirs, dv, small)
    )


def solution(mesh):
    split = P(("dp", "head"), None)
    line = P(("dp", "head"))
    return jax.shard_map(
        shards,
        mesh=mesh,
        in_specs=(split,) * 6 + (line, line, P()),
        out_specs=(split,) * 5,
        check_vma=False,
    )
```

time: 1110 us -> 102 us (0.09)
  the two profiles are of different devices: /device:TPU:250 before, /device:TPU:1 now
where the time goes in v1:
time: 102 us; the launch traced here: 101 us
  Pallas kernels  91.1 us (89%)
  local copies, waits for them, and re-layouts  7.17 us (7%)
  other arithmetic  2.07 us (2%)
    pallas_call x1, Pallas kernels, shards(): call(relay, [(square, F32)] * 2, [slots] * 4 + [dma((2, HOPS)), dma((2, H...  33.2 us
    pallas_call x1, Pallas kernels, shards(): call(exchange_out, [((ROWS, wide_out // 2), BF16), ((ROWS, wide_out // 2)...  22.5 us
    pallas_call x1, Pallas kernels, shards(): call(exchange_in, [(block_in, BF16)], [pltpu.VMEM(block_in, BF16), pltpu....  20.4 us
    pallas_call x1, Pallas kernels, shards(): call(local_first, [(square, F32)] * 4 + [(tall, F32)] * 4 + [(big, F32)]...  8.62 us
    unnamed x5, local copies, waits for them, and re-layouts  7.1 us
    pallas_call x1, Pallas kernels, shards(): call(local_second, [((2,) + tall, F32), (tall, BF16), (tall, BF16)], [plt...  6.34 us

profile of v1, /device:TPU:1, one launch (start us, length us, event | category | flops | bytes accessed | tf_op | source)
XLA Modules:
  0.0 101.0 jit_solution(8055670306383838808)
XLA Ops:
  0.6 0.7 convert_multiply_fusion
  1.3 0.1 broadcast_in_dim.2
  1.4 1.4 %pad_maximum_fusion.w_ref = f32[16,128]{1,0:T(8,128)} fusion(f32[16,64]{1,0:T(8,128)S(1)} %broadcast_in_dim.2, f32[16,32]{1,0:T(8,128)} %param.13, f32[16,32]{1,0:T(8,128)} %param.12), kind=kLoop, calls=%fused_computation | loop fusion | flops 4096 | bytes 16384 | tf_op jit(solution)/shard_map/concatenate | solution.py:422
  2.8 20.4 %exchange_in.1.in_ref = bf16[32,80,128]{2,1,0:T(8,128)(2,1)} custom-call(bf16[16,2048]{1,0:T(8,128)(2,1)} %q_ref.1, bf16[16,2048]{1,0:T(8,128)(2,1)} %k_ref.1, bf16[16,4096]{1,0:T(8,128)(2,1)} %v_ref.1, bf16[16,4096]{1,0:T(8,128)(2,1)} %g_ref.1, f32[16,128]{1,0:T(8,128)} %pad_maximum_fusion.w_ref), custom_call_target="tpu_custom_call" | custom-call | bytes 1048576 | tf_op jit(solution)/shard_map/exchange_in/pallas_call | solution.py:426
  23.2 8.6 %local_first.1 = (f32[128,128]{1,0:T(8,128)}, f32[128,128]{1,0:T(8,128)}, f32[128,128]{1,0:T(8,128)}, f32[128,128]{1,0:T(8,128)}, f32[512,128]{1,0:T(8,128)}, /*...) custom-call(s32[16]{0:T(128)} %lengths_ref.1, ...), custom_call_target="tpu_custom_call" | custom-call | bytes 1048576 | tf_op jit(solution)/shard_map/local_first/pallas_call | solution.py:434
  31.8 33.2 %relay.1 = (f32[128,128]{1,0:T(8,128)}, f32[128,128]{1,0:T(8,128)}) custom-call(f32[128,128]{1,0:T(8,128)} %get-tuple-element.21.phi_ref, f32[128,128]{1,0:T(8,128)} %get-tuple-element.22.phit_ref, f32[128,128]{1,0:T(8,128)} %get-tuple-element.23.bt_ref, f32[128,128]{1,0:T(8,128)} %get-tuple-element.24.lt_ref), custom_call_target="tpu_custom_call" | custom-call | bytes 1048576 | tf_op jit(solution)/shard_map/relay/pallas_call | solution.py:444
  65.1 6.3 %local_second.1 = (f32[2,512,128]{2,1,0:T(8,128)}, bf16[512,128]{1,0:T(8,128)(2,1)}, bf16[512,128]{1,0:T(8,128)(2,1)}) custom-call(bf16[32,80,128]{2,1,0:T(8,128)(2,1)} %exchange_in.1.in_ref, f32[128,128]{1,0:T(8,128)} %get-tuple-element.25.state_ref, f32[128,128]{1,0:T(8,128)} %get-tuple-element.26.grad_ref, f32[128,128]{1,0:T(8,128)} %get-tuple-element.22.phit_ref, ...), custom_call_target="tpu_custom_call" | custom-call | bytes 1048576 | tf_op jit(solution)/shard_map/local_second/pallas_call | solution.py:452
  71.4 22.5 %exchange_out.1 = (bf16[16,2048]{1,0:T(8,128)(2,1)}, bf16[16,2048]{1,0:T(8,128)(2,1)}, bf16[16,4096]{1,0:T(8,128)(2,1)}, f32[16,32]{1,0:T(8,128)}, f32[16,32]{1,0:T(8,128)}) custom-call(bf16[32,80,128]{2,1,0:T(8,128)(2,1)} %exchange_in.1.in_ref, f32[2,512,128]{2,1,0:T(8,128)} %get-tuple-element.34.dirs_ref, bf16[512,128]{1,0:T(8,128)(2,1)} %get-tuple-element.35.dv_ref, ...), custom_call_target="tpu_custom_call" | custom-call | bytes 1048576 | tf_op jit(solution)/shard_map/exchange_out/pallas_call | solution.py:462
  93.9 1.5 %copy.19 = bf16[16,2048]{1,0:T(8,128)(2,1)} copy(bf16[16,2048]{1,0:T(8,128)(2,1)} %get-tuple-element.42) | data formatting | bytes 131072
  95.4 1.5 %copy.20 = bf16[16,2048]{1,0:T(8,128)(2,1)} copy(bf16[16,2048]{1,0:T(8,128)(2,1)} %get-tuple-element.43) | data formatting | bytes 131072
  96.8 1.6 %copy.21 = bf16[16,4096]{1,0:T(8,128)(2,1)} copy(bf16[16,4096]{1,0:T(8,128)(2,1)} %get-tuple-element.44) | data formatting | bytes 262144
  98.4 1.3 %copy.22 = f32[16,32]{1,0:T(8,128)} copy(f32[16,32]{1,0:T(8,128)} %get-tuple-element.45) | data formatting | bytes 4096
  99.7 1.3 %copy.23 = f32[16,32]{1,0:T(8,128)} copy(f32[16,32]{1,0:T(8,128)} %get-tuple-element.46) | data formatting | bytes 4096

commit v2 on v1

v2 whole, which is shorter than its diff:
```python
import jax
import jax.numpy as jnp
from jax import lax
from jax.experimental import pallas as pl
from jax.experimental.pallas import tpu as pltpu
from jax.sharding import PartitionSpec as P

HEAD_DIM = 128
TILE = 128
HEADS = 32
ROWS = 16
SPAN = HEADS * ROWS
TILES = SPAN // TILE
REACH = (1, 2, 3)
NDOCS = 16
SCALE = HEAD_DIM ** (-0.5)
MESH = pl.DeviceIdType.MESH
F32 = jnp.float32
BF16 = jnp.bfloat16
LIMIT = 56 * 1024 * 1024


def product(left, right, over=(1, 0)):
    return lax.dot_general(
        left, right, (((over[0],), (over[1],)), ((), ())), preferred_element_type=F32
    )


def halves(values):
    high = values.astype(BF16)
    return high, (values - high.astype(F32)).astype(BF16)


def thirds(values):
    high, rest = values.astype(BF16), None
    rest = values - high.astype(F32)
    middle = rest.astype(BF16)
    return high, middle, (rest - middle.astype(F32)).astype(BF16)


def product3(left, right, over=(1, 0)):
    (lh, ll), (rh, rl) = left, right
    return product(lh, rh, over) + (product(lh, rl, over) + product(ll, rh, over))


def product2l(left, right, over=(1, 0)):
    return product(left[0], right, over) + product(left[1], right, over)


def product2r(left, right, over=(1, 0)):
    return product(left, right[0], over) + product(left, right[1], over)


def iota(shape, axis):
    return lax.broadcasted_iota(jnp.int32, shape, axis)


def band(index):
    return slice(index * TILE, (index + 1) * TILE)


def place():
    dp, head = lax.axis_index("dp"), lax.axis_index("head")
    base = lax.div(dp, 4) * 4
    me = lax.rem(dp, 4) * 8 + head

    def device(index):
        return (base + lax.div(index, 8), lax.rem(index, 8))

    return dp, head, me, device


def greet_plane(me, device):
    barrier = pltpu.get_barrier_semaphore()

    def greet(offset, carry):
        target = lax.rem(me + offset, HEADS)
        pl.semaphore_signal(barrier, inc=1, device_id=device(target), device_id_type=MESH)
        return carry

    lax.fori_loop(1, HEADS, greet, 0)
    return barrier


def start_plane(me, device, sent, landed, send_sem, recv_sem):
    def send(offset, carry):
        target = lax.rem(me + offset, HEADS)
        pltpu.make_async_remote_copy(
            src_ref=sent.at[target],
            dst_ref=landed.at[me],
            send_sem=send_sem,
            recv_sem=recv_sem,
            device_id=device(target),
            device_id_type=MESH,
        ).start()
        return carry

    lax.fori_loop(1, HEADS, send, 0)
    landed[me] = sent[me]


def finish_plane(sent, landed, send_sem, recv_sem):
    others = pl.ds(0, HEADS - 1)
    pltpu.make_async_copy(sent.at[others], landed.at[others], recv_sem).wait()
    pltpu.make_async_copy(sent.at[others], landed.at[others], send_sem).wait()


def raw_parts(landed):
    return [landed[:, n * 16 : n * 16 + 16, :].reshape(SPAN, TILE) for n in range(5)]


def whole(
    q_ref, k_ref, v_ref, g_ref, beta_ref, decay_ref, ratio_ref, clip_ref, lengths_ref,
    out_ref,
    sent_in, in_ref, columns_ref, lower_ref, upper_ref, start_ref, end_ref,
    u0_ref, wk_ref, x0_ref, xk_ref, gqk_ref, gkk_ref, a_ref, pw_ref, th_ref, tl_ref,
    fqh_ref, fql_ref, fkh_ref, fkl_ref, dirs_ref, partner_in, sent_out, landed,
    maps_out, maps_in, far_out, far_in, plane_send, plane_recv, out_send, out_recv,
    pair_send, pair_recv, map_send, map_recv,
):
    dp, head, me, device = place()
    count, core = lax.axis_size("dp"), lax.rem(head, 2)

    def along(distance):
        return (lax.rem(dp + (count + 4 * distance), count), head)

    barrier = greet_plane(me, device)
    for distance in REACH:
        for sign in (1, -1):
            pl.semaphore_signal(
                barrier, inc=1, device_id=along(sign * distance), device_id_type=MESH
            )

    columns_ref[...] = jnp.zeros((ROWS, TILE), F32)
    columns_ref[:, 0:32] = beta_ref[...]
    columns_ref[:, 32:64] = decay_ref[...]
    weight = ratio_ref[...] * clip_ref[...].astype(F32)
    diagonal = iota((ROWS, ROWS), 0) == iota((ROWS, ROWS), 1)
    weight = jnp.sum(jnp.where(diagonal, jnp.broadcast_to(weight, (ROWS, ROWS)), 0.0), axis=1, keepdims=True)
    wide = iota((ROWS, TILE), 1) >= 64
    columns = jnp.where(wide, jnp.broadcast_to(weight, (ROWS, TILE)), columns_ref[...])
    parts = [p.astype(F32) for p in thirds(columns)]
    lane = iota((ROWS, TILE), 1) % 32
    for j in range(HEADS):
        pair = slice((j // 2) * HEAD_DIM, (j // 2 + 1) * HEAD_DIM)
        own = slice(j * HEAD_DIM, (j + 1) * HEAD_DIM)
        sent_in[j, 0:16, :] = q_ref[:, pair]
        sent_in[j, 16:32, :] = k_ref[:, pair]
        sent_in[j, 32:48, :] = v_ref[:, own]
        sent_in[j, 48:64, :] = g_ref[:, own]
        small = jnp.zeros((ROWS, TILE), F32)
        for n in range(3):
            moved = pltpu.roll(parts[n], (TILE - j + n) % TILE, 1)
            small = jnp.where(lane == n, moved, small)
        sent_in[j, 64:80, :] = small.astype(BF16)
    pl.semaphore_wait(barrier, HEADS - 1 + 2 * len(REACH))
    start_plane(me, device, sent_in, in_ref, plane_send, plane_recv)

    base = lax.div(dp, 4) * SPAN
    lower_ref[...] = (iota((SPAN, SPAN), 0) >= iota((SPAN, SPAN), 1)).astype(F32).astype(BF16)
    upper_ref[...] = (iota((SPAN, SPAN), 0) <= iota((SPAN, SPAN), 1)).astype(F32).astype(BF16)
    start = jnp.full((SPAN, TILE), -base, jnp.int32)
    row = iota((SPAN, TILE), 0)
    bound, last_start = -base, -base
    for n in range(NDOCS - 1):
        bound = bound + lengths_ref[n]
        start = jnp.where(row >= bound, bound, start)
        last_start = jnp.where(bound <= SPAN - 1, bound, last_start)
    start_ref[...] = start
    end_ref[...] = (row >= last_start).astype(F32)
    for size in (TILE, 2 * TILE):
        for n in range(SPAN // (2 * size)):
            top = slice(2 * n * size, (2 * n + 1) * size)
            low = slice((2 * n + 1) * size, (2 * n + 2) * size)
            th_ref[top, low] = jnp.zeros((size, size), BF16)
            tl_ref[top, low] = jnp.zeros((size, size), BF16)
    finish_plane(sent_in, in_ref, plane_send, plane_recv)

    qr, kr, vr, gr, small = raw_parts(in_ref)
    qf, kf = qr.astype(F32), kr.astype(F32)
    pick_row, pick_col = iota((TILE, 3 * TILE), 0), iota((TILE, 3 * TILE), 1)
    pick = (pick_row // 32 == pick_col // TILE) & (pick_row % 32 < 3)
    spread = product(small, pick.astype(F32).astype(BF16))
    beta = jax.nn.sigmoid(spread[:, 0:TILE])
    weight = spread[:, 2 * TILE :]
    sk = lax.rsqrt(jnp.sum(kf * kf, axis=1, keepdims=True) + 1e-06)
    sk = jnp.broadcast_to(sk, (SPAN, TILE))
    csw = lax.rsqrt(jnp.sum(qf * qf, axis=1, keepdims=True) + 1e-06) * SCALE * weight
    running = product(lower_ref[...], small)
    lane = iota((SPAN, TILE), 1)
    running = jnp.where(lane // 32 == 1, running, 0.0)
    cumul = -jnp.broadcast_to(jnp.sum(running, axis=1, keepdims=True), (SPAN, TILE))
    start = start_ref[...]
    gamma = jnp.where(start < 0, jnp.exp(cumul), 0.0)
    last = cumul[SPAN - 1 : SPAN, :]
    end = end_ref[...] * jnp.exp(jnp.minimum(last - cumul, 0.0))
    pack = jnp.where(lane == 0, cumul, jnp.where(lane == 1, sk, 0.0))
    across = jnp.transpose(pack)
    tok, src = iota((TILE, TILE), 0), iota((TILE, TILE), 1)
    for i in range(TILES):
        bi = band(i)
        for j in range(i + 1):
            bj = band(j)
            gap = cumul[bi] - across[0:1, bj]
            seen = src + j * TILE >= start[bi]
            if i == j:
                seen = seen & (tok >= src)
            pair = jnp.where(seen, jnp.exp(jnp.minimum(gap, 0.0)), 0.0) * across[1:2, bj]
            gqk = pair * csw[bi]
            gkk = pair * (beta[bi] * sk[bi])
            if i == j:
                gkk = jnp.where(tok > src, gkk, 0.0)
            gqk_ref[bi, bj] = gqk
            gkk_ref[bi, bj] = gkk
            a_ref[bi, bj] = gkk * product(kr[bi], kr[bj], (1, 1))
            pw_ref[bi, bj] = gqk * product(qr[bi], kr[bj], (1, 1))
    eye = (tok == src).astype(F32)
    inverse = [
        eye - jnp.where(tok // 2 == src // 2, a_ref[band(i), band(i)], 0.0) for i in range(TILES)
    ]
    size = 2
    while size < TILE:
        inside = (tok // (2 * size) == src // (2 * size)) & (tok // size != src // size)
        for i in range(TILES):
            block = halves(jnp.where(inside, a_ref[band(i), band(i)], 0.0))
            parts = halves(inverse[i])
            inverse[i] = inverse[i] - product3(parts, halves(product3(block, parts)))
        size *= 2
    for i in range(TILES):
        th_ref[band(i), band(i)], tl_ref[band(i), band(i)] = halves(inverse[i])
    while size < SPAN:
        for n in range(SPAN // (2 * size)):
            top = slice(2 * n * size, (2 * n + 1) * size)
            low = slice((2 * n + 1) * size, (2 * n + 2) * size)
            right = product3(halves(a_ref[low, top]), (th_ref[top, top], tl_ref[top, top]))
            block = -product3((th_ref[low, low], tl_ref[low, low]), halves(right))
            th_ref[low, top], tl_ref[low, top] = halves(block)
        size *= 2
    keys = sk * kf
    rhs = halves(jnp.concatenate([beta * vr.astype(F32), beta * gamma * keys], axis=1))
    solved = []
    for i in range(TILES):
        bi, upto = band(i), slice(0, (i + 1) * TILE)
        part = product3((th_ref[bi, upto], tl_ref[bi, upto]), (rhs[0][upto], rhs[1][upto]))
        u0_ref[bi] = part[:, :TILE]
        wk_ref[bi] = part[:, TILE:]
        solved.append(part)
    solved = halves(jnp.concatenate(solved, axis=0))
    end_keys = end * keys
    both = product3(solved, halves(end_keys), (0, 0))
    phit = gamma[SPAN - 1 : SPAN, :] * eye - both[TILE:]
    wks = (solved[0][:, TILE:], solved[1][:, TILE:])
    reads = []
    for i in range(TILES):
        bi, upto = band(i), slice(0, (i + 1) * TILE)
        part = product3(halves(pw_ref[bi, upto]), (wks[0][upto], wks[1][upto]))
        reads.append(gamma[bi] * csw[bi] * qf[bi] - part)
    lt = product2r(gr, halves(jnp.concatenate(reads, axis=0)), (0, 0))

    def ship(way, number, source, target, distance):
        copy = pltpu.make_async_remote_copy(
            src_ref=source,
            dst_ref=target,
            send_sem=map_send.at[way, number],
            recv_sem=map_recv.at[way, number],
            device_id=along(distance if way == 0 else -distance),
            device_id_type=MESH,
        )
        copy.start()
        return copy

    copies = []
    maps_out[0, 0, 0:TILE] = phit
    maps_out[0, 0, TILE:] = both[:TILE]
    maps_out[1, 0, 0:TILE] = jnp.transpose(phit)
    maps_out[1, 0, TILE:] = lt
    for way in range(2):
        copies.append(ship(way, 0, maps_out.at[way, 0], maps_in.at[way, 0], 1))
    pulled = []
    for j in range(TILES):
        bj, onward = band(j), slice(j * TILE, SPAN)
        pulled.append(product2l(halves(pw_ref[onward, bj]), gr[onward], (0, 0)))
    pulled = halves(jnp.concatenate([jnp.concatenate(pulled, axis=0), end_keys], axis=1))
    for j in range(TILES):
        bj, onward = band(j), slice(j * TILE, SPAN)
        part = product3(
            (th_ref[onward, bj], tl_ref[onward, bj]), (pulled[0][onward], pulled[1][onward]), (0, 0)
        )
        x0_ref[bj] = part[:, :TILE]
        xk_ref[bj] = part[:, TILE:]
    steps = []
    for way in range(2):
        copies[way].wait_recv()
        own = maps_out[way, 0]
        joined = product3(halves(maps_in[way, 0]), halves(own[:TILE]))
        maps_out[way, 1, 0:TILE] = joined[:TILE]
        maps_out[way, 1, TILE:] = joined[TILE:] + own[TILE:]
        copies.append(ship(way, 1, maps_out.at[way, 1, pl.ds(TILE, TILE)], far_in.at[way, 0], 2))
        steps.append(halves(maps_out[way, 1, 0:TILE]))
    for way in range(2):
        copies.append(ship(way, 4, maps_out.at[way, 1], maps_in.at[way, 1], 1))
    for level in range(2):
        for way in range(2):
            copies[2 + way + 4 * level].wait_recv()
            reached = product3(halves(far_in[way, level]), steps[way])
            far_out[way, level] = reached + maps_out[way, 1, TILE:]
            copies.append(
                ship(way, 2 + level, far_out.at[way, level], far_in.at[way, level + 1], 2 + level)
            )
    ends = []
    for way in range(2):
        copies[4 + way].wait_recv()
        near = maps_in[way, 1]
        step = halves(near[:TILE])
        copies[8 + way].wait_recv()
        ends.append(product3(halves(far_in[way, 2]), step) + near[TILE:])
    state, grad = halves(ends[0]), halves(ends[1])

    u = u0_ref[...] - product3(halves(wk_ref[...]), state, (1, 1))
    x = x0_ref[...] + product3(halves(xk_ref[...]), grad, (1, 1))
    dv = beta * x
    sent_out[:, 16:32, :] = dv.astype(BF16).reshape(HEADS, ROWS, TILE)
    (uh, ul), (xh, xl) = halves(u), halves(x)
    for i in range(TILES):
        bi = band(i)
        for j in range(i + 1):
            bj = band(j)
            read = product2r(gr[bi], (uh[bj], ul[bj]), (1, 1))
            solve = product3((xh[bi], xl[bi]), (uh[bj], ul[bj]), (1, 1))
            fqh_ref[bi, bj], fql_ref[bi, bj] = halves(gqk_ref[bi, bj] * read)
            fkh_ref[bi, bj], fkl_ref[bi, bj] = halves(-gkk_ref[bi, bj] * solve)
    dq = csw * gamma * product2r(gr, state)
    dk = end * sk * product3((uh, ul), grad) - beta * gamma * sk * product3((xh, xl), state)
    for i in range(TILES):
        bi, upto, onward = band(i), slice(0, (i + 1) * TILE), slice(i * TILE, SPAN)
        dirs_ref[0, bi] = dq[bi] + product2l((fqh_ref[bi, upto], fql_ref[bi, upto]), kr[upto])
        part = product2l((fqh_ref[onward, bi], fql_ref[onward, bi]), qr[onward], (0, 0))
        part = part + product2l((fkh_ref[onward, bi], fkl_ref[onward, bi]), kr[onward], (0, 0))
        part = part + product2l((fkh_ref[bi, upto], fkl_ref[bi, upto]), kr[upto])
        dirs_ref[1, bi] = dk[bi] + part
    pair = pltpu.make_async_remote_copy(
        src_ref=dirs_ref.at[1 - core],
        dst_ref=partner_in,
        send_sem=pair_send,
        recv_sem=pair_recv,
        device_id=(dp, head + 1 - 2 * core),
        device_id_type=MESH,
    )
    pair.start()
    after = product3(state, halves(phit)) + both[:TILE]
    total = jnp.sum(jnp.sum(ends[1] * after, axis=1, keepdims=True), axis=0, keepdims=True)
    xu = jnp.sum(x * u, axis=1, keepdims=True)
    change = jnp.sum(
        qf * dirs_ref[0] - kf * dirs_ref[1] - 2.0 * (vr.astype(F32) * dv), axis=1, keepdims=True
    )
    change = change + 2.0 * xu
    change = jnp.where(iota((SPAN, 1), 0) == SPAN - 1, change + total, change)
    pieces = [p.astype(F32) for p in thirds(jnp.broadcast_to(change, (SPAN, TILE)))]
    packed = jnp.zeros((SPAN, TILE), F32)
    for n in range(3):
        packed = jnp.where(lane == n, pieces[n], packed)
    ddecay = -jnp.sum(product(upper_ref[...], packed.astype(BF16)), axis=1, keepdims=True)
    ddecay = jnp.broadcast_to(ddecay, (SPAN, TILE))
    out = jnp.zeros((SPAN, TILE), F32)
    for n, values in enumerate((xu * (1.0 - beta), ddecay)):
        high, low = halves(values)
        out = jnp.where(lane == me + 32 * n, high.astype(F32), out)
        out = jnp.where(lane == me + 32 * n + 64, low.astype(F32), out)
    sent_out[:, 32:48, :] = out.astype(BF16).reshape(HEADS, ROWS, TILE)
    own = jnp.where(core == 0, qf, kf)
    inverse = 1.0 / (jnp.sum(own * own, axis=1, keepdims=True) + 1e-06)
    pair.wait_recv()
    part = dirs_ref[core] + partner_in[...]
    part = part - own * (jnp.sum(own * part, axis=1, keepdims=True) * inverse)
    sent_out[:, 0:16, :] = part.astype(BF16).reshape(HEADS, ROWS, TILE)
    start_plane(me, device, sent_out, landed, out_send, out_recv)
    for one in copies:
        one.wait_send()
    pair.wait_send()
    finish_plane(sent_out, landed, out_send, out_recv)
    out_ref[...] = landed[...]


def unpack(in_ref, dq_ref, dk_ref, dv_ref, db_ref, dd_ref):
    total = jnp.zeros((ROWS, TILE), F32)
    for j in range(HEADS):
        to_ref = (dq_ref, dk_ref)[j % 2]
        to_ref[:, (j // 2) * HEAD_DIM : (j // 2 + 1) * HEAD_DIM] = in_ref[j, 0:16, :]
        dv_ref[:, j * HEAD_DIM : (j + 1) * HEAD_DIM] = in_ref[j, 16:32, :]
        total = total + in_ref[j, 32:48, :].astype(F32)
    total = total + pltpu.roll(total, 64, 1)
    db_ref[...] = total[:, 0:32]
    dd_ref[...] = total[:, 32:64]


def shards(query, key, value, beta_logit, decay, out_grad, ratio, clip_mask, lengths):
    dma = pltpu.SemaphoreType.DMA
    vmem, smem = [pl.BlockSpec(memory_space=m) for m in (pltpu.VMEM, pltpu.SMEM)]
    square, tall, big = (TILE, TILE), (SPAN, TILE), (SPAN, SPAN)
    block_in, block_out, double = (HEADS, 80, TILE), (HEADS, 48, TILE), (2 * TILE, TILE)
    blocks = pl.pallas_call(
        whole,
        out_shape=jax.ShapeDtypeStruct(block_out, BF16),
        in_specs=[vmem] * 8 + [smem],
        out_specs=vmem,
        scratch_shapes=[
            pltpu.VMEM(block_in, BF16),
            pltpu.VMEM(block_in, BF16),
            pltpu.VMEM((ROWS, TILE), F32),
            pltpu.VMEM(big, BF16),
            pltpu.VMEM(big, BF16),
            pltpu.VMEM(tall, jnp.int32),
            pltpu.VMEM(tall, F32),
        ]
        + [pltpu.VMEM(tall, F32)] * 4
        + [pltpu.VMEM(big, F32)] * 4
        + [pltpu.VMEM(big, BF16)] * 6
        + [
            pltpu.VMEM((2,) + tall, F32),
            pltpu.VMEM(tall, F32),
            pltpu.VMEM(block_out, BF16),
            pltpu.VMEM(block_out, BF16),
            pltpu.VMEM((2, 2) + double, F32),
            pltpu.VMEM((2, 2) + double, F32),
            pltpu.VMEM((2, 2) + square, F32),
            pltpu.VMEM((2, 3) + square, F32),
        ]
        + [dma] * 6
        + [dma((2, 5)), dma((2, 5))],
        compiler_params=pltpu.CompilerParams(
            vmem_limit_bytes=LIMIT, collective_id=0, has_side_effects=True
        ),
        cost_estimate=pl.CostEstimate(flops=1 << 30, bytes_accessed=1 << 20, transcendentals=0),
        name="whole",
    )(
        query, key, value, out_grad, beta_logit, decay,
        ratio.reshape(1, ROWS), clip_mask.reshape(1, ROWS), lengths,
    )
    wide = HEADS * HEAD_DIM
    shapes = [((ROWS, wide // 2), BF16)] * 2 + [((ROWS, wide), BF16)] + [((ROWS, HEADS), F32)] * 2
    return tuple(
        pl.pallas_call(
            unpack,
            out_shape=[jax.ShapeDtypeStruct(s, d) for s, d in shapes],
            in_specs=[vmem],
            out_specs=[vmem] * 5,
            compiler_params=pltpu.CompilerParams(vmem_limit_bytes=LIMIT),
            cost_estimate=pl.CostEstimate(flops=0, bytes_accessed=1 << 20, transcendentals=0),
            name="unpack",
        )(blocks)
    )


def solution(mesh):
    split = P(("dp", "head"), None)
    line = P(("dp", "head"))
    return jax.shard_map(
        shards,
        mesh=mesh,
        in_specs=(split,) * 6 + (line, line, P()),
        out_specs=(split,) * 5,
        check_vma=False,
    )
```

time: 102 us -> 69.2 us (0.68)
  Pallas kernels: 91.1 us -> 68.4 us
  local copies, waits for them, and re-layouts: 7.17 us -> 0 us
  other arithmetic: 2.07 us -> 0 us
    pallas_call x5 -> x2, Pallas kernels: 91.1 us -> 68.4 us  [the longest x1 66.6 us: shards(): pl.pallas_call(whole, out_shape=jax.ShapeDtypeStruct(block_out, BF16), in...]
    unnamed x5 -> x0, local copies, waits for them, and re-layouts: 7.1 us -> none
    concatenate x1 -> x0, other arithmetic: 1.39 us -> none  [shards(): columns = jnp.concatenate([beta_logit, decay, wide], axis=1)]
where the time goes in v2:
time: 69.2 us; the launch traced here: 69.1 us
  Pallas kernels  68.4 us (99%)
    pallas_call x1, Pallas kernels, shards(): pl.pallas_call(whole, out_shape=jax.ShapeDtypeStruct(block_out, BF16), in...  66.6 us
    pallas_call x1, Pallas kernels, shards(): pl.pallas_call(unpack, out_shape=[jax.ShapeDtypeStruct(s, d) for s, d in...  1.79 us

profile of v2, /device:TPU:1, one launch (start us, length us, event | category | flops | bytes accessed | tf_op | source)
XLA Modules:
  0.0 69.1 jit_solution(17186531263019609662)
XLA Ops:
  0.6 66.6 %whole.1.in_ref = bf16[32,48,128]{2,1,0:T(8,128)(2,1)} custom-call(bf16[16,2048]{1,0:T(8,128)(2,1)} %q_ref.1, bf16[16,2048]{1,0:T(8,128)(2,1)} %k_ref.1, bf16[16,4096]{1,0:T(8,128)(2,1)} %v_ref.1, bf16[16,4096]{1,0:T(8,128)(2,1)} %g_ref.1, f32[16,32]{1,0:T(8,128)} %beta_ref.1, f32[16,32]{1,0:T(8,128)} %decay_ref.1, f32[1,16]{1,0:T(1,128)} %bitcast.2, ...), custom_call_target="tpu_custom_call" | custom-call | flops 1073741824 | bytes 1048576 | tf_op jit(solution)/shard_map/whole/pallas_call | solution.py:401
  67.3 1.8 %unpack.1 = (bf16[16,2048]{1,0:T(8,128)(2,1)}, bf16[16,2048]{1,0:T(8,128)(2,1)}, bf16[16,4096]{1,0:T(8,128)(2,1)}, f32[16,32]{1,0:T(8,128)}, f32[16,32]{1,0:T(8,128)}) custom-call(bf16[32,48,128]{2,1,0:T(8,128)(2,1)} %whole.1.in_ref), custom_call_target="tpu_custom_call" | custom-call | bytes 1048576 | tf_op jit(solution)/shard_map/unpack/pallas_call | solution.py:442

commit v3 on v0

v3 whole, which is shorter than its diff:
```python
import jax
import jax.numpy as jnp
from jax import lax
from jax.experimental import pallas as pl
from jax.experimental.pallas import tpu as pltpu
from jax.sharding import PartitionSpec as P

HEAD_DIM = 128
TILE = 128
HEADS = 32
ROWS = 16
SPAN = HEADS * ROWS
TILES = SPAN // TILE
HALF = SPAN // 2
CHUNKS = 4
REACH = (1, 2)
NDOCS = 16
SCALE = HEAD_DIM ** (-0.5)
MESH = pl.DeviceIdType.MESH
F32 = jnp.float32
BF16 = jnp.bfloat16
LIMIT = 56 * 1024 * 1024


def product(left, right, over=(1, 0)):
    return lax.dot_general(
        left, right, (((over[0],), (over[1],)), ((), ())), preferred_element_type=F32
    )


def halves(values):
    high = values.astype(BF16)
    return high, (values - high.astype(F32)).astype(BF16)


def thirds(values):
    high = values.astype(BF16)
    rest = values - high.astype(F32)
    middle = rest.astype(BF16)
    return high, middle, (rest - middle.astype(F32)).astype(BF16)


def joined(parts, axis):
    return jnp.concatenate(parts, axis=axis)


def product3(left, right, over=(1, 0)):
    (lh, ll), (rh, rl) = left, right
    return product(joined([lh, ll, lh], over[0]), joined([rh, rh, rl], over[1]), over)


def product2l(left, right, over=(1, 0)):
    return product(joined(left, over[0]), joined([right, right], over[1]), over)


def product2r(left, right, over=(1, 0)):
    return product(joined([left, left], over[0]), joined(right, over[1]), over)


def iota(shape, axis):
    return lax.broadcasted_iota(jnp.int32, shape, axis)


def band(index, size=TILE):
    return slice(index * size, (index + 1) * size)


def place():
    dp, head = lax.axis_index("dp"), lax.axis_index("head")
    base = lax.div(dp, 4) * 4
    me = lax.rem(dp, 4) * 8 + head

    def device(index):
        return (base + lax.div(index, 8), lax.rem(index, 8))

    return dp, head, me, device


def greet_plane(me, device):
    barrier = pltpu.get_barrier_semaphore()

    def greet(offset, carry):
        target = lax.rem(me + offset, HEADS)
        pl.semaphore_signal(barrier, inc=1, device_id=device(target), device_id_type=MESH)
        return carry

    lax.fori_loop(1, HEADS, greet, 0)
    return barrier


def start_plane(me, device, kinds):
    def send(offset, carry):
        target = lax.rem(me + 7 * offset, HEADS)
        for sent, landed, send_sem, recv_sem in kinds:
            pltpu.make_async_remote_copy(
                src_ref=sent.at[target],
                dst_ref=landed.at[me],
                send_sem=send_sem,
                recv_sem=recv_sem,
                device_id=device(target),
                device_id_type=MESH,
            ).start()
        return carry

    lax.fori_loop(1, HEADS, send, 0)
    for sent, landed, _, _ in kinds:
        landed[me] = sent[me]


def await_sent(kinds):
    others = pl.ds(0, HEADS - 1)
    for sent, landed, send_sem, _ in kinds:
        pltpu.make_async_copy(sent.at[others], landed.at[others], send_sem).wait()


def await_landed(kinds):
    others = pl.ds(0, HEADS - 1)
    for sent, landed, _, recv_sem in kinds:
        pltpu.make_async_copy(sent.at[others], landed.at[others], recv_sem).wait()


def rows_of(landed):
    return landed.reshape(SPAN, TILE)


def prepare(base, lengths_ref, m):
    down, along = iota((SPAN, SPAN), 0), iota((SPAN, SPAN), 1)
    m.lower[...] = (down >= along).astype(F32).astype(BF16)
    m.upper[...] = (down <= along).astype(F32).astype(BF16)
    down, along = iota((HEADS, SPAN), 0), iota((HEADS, SPAN), 1)
    m.fold[...] = (down == along // ROWS).astype(F32).astype(BF16)
    down, along = iota((SPAN, HEADS), 0), iota((SPAN, HEADS), 1)
    m.unfold[...] = (down // ROWS == along).astype(F32).astype(BF16)
    start = jnp.full((SPAN, TILE), -base, jnp.int32)
    row = iota((SPAN, TILE), 0)
    bound, last_start = -base, -base
    for n in range(NDOCS - 1):
        bound = bound + lengths_ref[n]
        start = jnp.where(row >= bound, bound, start)
        last_start = jnp.where(bound <= SPAN - 1, bound, last_start)
    m.start[...] = start
    m.end[...] = (row >= last_start).astype(F32)
    for size in (TILE, HALF):
        for n in range(SPAN // (2 * size)):
            top, low = band(2 * n, size), band(2 * n + 1, size)
            m.th[top, low] = jnp.zeros((size, size), BF16)
            m.tl[top, low] = jnp.zeros((size, size), BF16)


def first_keys(m):
    kr = rows_of(m.k_in[...])
    kf = kr.astype(F32)
    lane, row = iota((SPAN, TILE), 1), iota((SPAN, TILE), 0)
    high, low = halves(m.rows_in[:, 0, :])
    packed = (high.astype(F32) + pltpu.roll(low.astype(F32), 64, 1)).astype(BF16)
    small = product(m.unfold[...], packed)
    small = jnp.where(lane % ROWS == row % ROWS, small, 0.0).astype(BF16)
    pick_row, pick_col = iota((TILE, 3 * TILE), 0), iota((TILE, 3 * TILE), 1)
    pick = ((pick_row // ROWS) % 4 == pick_col // TILE).astype(F32).astype(BF16)
    spread = product(small, pick)
    beta = jax.nn.sigmoid(spread[:, 0:TILE])
    m.weight[...] = spread[:, 2 * TILE :]
    sk = lax.rsqrt(jnp.sum(kf * kf, axis=1, keepdims=True) + 1e-06)
    sk = jnp.broadcast_to(sk, (SPAN, TILE))
    running = product(m.lower[...], small)
    running = jnp.where((lane // ROWS) % 4 == 1, running, 0.0)
    cumul = -jnp.broadcast_to(jnp.sum(running, axis=1, keepdims=True), (SPAN, TILE))
    start = m.start[...]
    gamma = jnp.where(start < 0, jnp.exp(cumul), 0.0)
    last = cumul[SPAN - 1 : SPAN, :]
    m.end[...] = m.end[...] * jnp.exp(jnp.minimum(last - cumul, 0.0))
    m.beta[...] = beta
    m.gamma[...] = gamma
    m.sk[...] = sk
    pack = jnp.where(lane == 0, cumul, jnp.where(lane == 1, sk, 0.0))
    across = jnp.transpose(pack)
    tok, src = iota((TILE, TILE), 0), iota((TILE, TILE), 1)
    for i in range(TILES):
        bi = band(i)
        for j in range(i + 1):
            bj = band(j)
            gap = cumul[bi] - across[0:1, bj]
            seen = src + j * TILE >= start[bi]
            if i == j:
                seen = seen & (tok >= src)
            pair = jnp.where(seen, jnp.exp(jnp.minimum(gap, 0.0)), 0.0) * across[1:2, bj]
            gkk = pair * (beta[bi] * sk[bi])
            if i == j:
                gkk = jnp.where(tok > src, gkk, 0.0)
            m.gqk[bi, bj] = pair
            m.gkk[bi, bj] = gkk
            m.a[bi, bj] = gkk * product(kr[bi], kr[bj], (1, 1))
    eye = (tok == src).astype(F32)
    inverse = [
        eye - jnp.where(tok // 2 == src // 2, m.a[band(i), band(i)], 0.0) for i in range(TILES)
    ]
    size = 2
    while size < TILE:
        inside = (tok // (2 * size) == src // (2 * size)) & (tok // size != src // size)
        for i in range(TILES):
            block = halves(jnp.where(inside, m.a[band(i), band(i)], 0.0))
            parts = halves(inverse[i])
            inverse[i] = inverse[i] - product3(parts, halves(product3(block, parts)))
        size *= 2
    for i in range(TILES):
        m.th[band(i), band(i)], m.tl[band(i), band(i)] = halves(inverse[i])


def first_state(m):
    kr, vr = rows_of(m.k_in[...]), rows_of(m.v_in[...])
    beta, gamma = m.beta[...], m.gamma[...]
    size = TILE
    while size < SPAN:
        for n in range(SPAN // (2 * size)):
            top, low = band(2 * n, size), band(2 * n + 1, size)
            right = product3(halves(m.a[low, top]), (m.th[top, top], m.tl[top, top]))
            block = -product3((m.th[low, low], m.tl[low, low]), halves(right))
            m.th[low, top], m.tl[low, top] = halves(block)
        size *= 2
    keys = m.sk[...] * kr.astype(F32)
    rhs = halves(joined([beta * vr.astype(F32), beta * gamma * keys], 1))
    solved = []
    for i in range(2):
        bi, upto = band(i, HALF), slice(0, (i + 1) * HALF)
        part = product3((m.th[bi, upto], m.tl[bi, upto]), (rhs[0][upto], rhs[1][upto]))
        m.u0[bi] = part[:, :TILE]
        m.wk[bi] = part[:, TILE:]
        solved.append(part)
    ends = halves(m.end[...] * keys)
    m.zh[:, TILE:], m.zl[:, TILE:] = ends
    both = product3(halves(joined(solved, 0)), ends, (0, 0))
    eye = (iota((TILE, TILE), 0) == iota((TILE, TILE), 1)).astype(F32)
    return gamma[SPAN - 1 : SPAN, :] * eye - both[TILE:], both[:TILE]


def first_grad(m):
    kr, qr, gr = [rows_of(r[...]) for r in (m.k_in, m.q_in, m.g_in)]
    qf = qr.astype(F32)
    csw = lax.rsqrt(jnp.sum(qf * qf, axis=1, keepdims=True) + 1e-06) * SCALE * m.weight[...]
    m.csw[...] = csw
    for i in range(TILES):
        bi = band(i)
        for j in range(i + 1):
            bj = band(j)
            gqk = m.gqk[bi, bj] * csw[bi]
            m.gqk[bi, bj] = gqk
            m.ph[bi, bj], m.pl[bi, bj] = halves(gqk * product(qr[bi], kr[bj], (1, 1)))
    for j in range(TILES):
        bj, onward = band(j), slice(j * TILE, SPAN)
        pulled = product2l((m.ph[onward, bj], m.pl[onward, bj]), gr[onward], (0, 0))
        m.zh[bj, :TILE], m.zl[bj, :TILE] = halves(pulled)
    reads = product2r(gr, halves(m.gamma[...] * csw * qf), (0, 0))
    return reads - product3((m.zh[:, :TILE], m.zl[:, :TILE]), halves(m.wk[...]), (0, 0))


def first_beside(m):
    for j in range(2):
        bj, onward = band(j, HALF), slice(j * HALF, SPAN)
        part = product3((m.th[onward, bj], m.tl[onward, bj]), (m.zh[onward], m.zl[onward]), (0, 0))
        m.x0[bj] = part[:, :TILE]
        m.xk[bj] = part[:, TILE:]


def second(m, state_t, grad_t, phit, bt, send_values, send_directions, finish_directions, send_rows):
    kr, qr, vr, gr = [rows_of(r[...]) for r in (m.k_in, m.q_in, m.v_in, m.g_in)]
    beta, gamma, sk, csw, end = m.beta[...], m.gamma[...], m.sk[...], m.csw[...], m.end[...]
    state, grad = halves(state_t), halves(grad_t)
    x = m.x0[...] + product3(halves(m.xk[...]), grad, (1, 1))
    dv = beta * x
    send_values(dv)
    u = m.u0[...] - product3(halves(m.wk[...]), state, (1, 1))
    (uh, ul), (xh, xl) = halves(u), halves(x)
    for i in range(TILES):
        bi = band(i)
        for j in range(i + 1):
            bj = band(j)
            read = product2r(gr[bi], (uh[bj], ul[bj]), (1, 1))
            solve = product3((xh[bi], xl[bi]), (uh[bj], ul[bj]), (1, 1))
            m.fqh[bi, bj], m.fql[bi, bj] = halves(m.gqk[bi, bj] * read)
            m.fkh[bi, bj], m.fkl[bi, bj] = halves(-m.gkk[bi, bj] * solve)
    dq = csw * gamma * product2r(gr, state)
    dk = end * sk * product3((uh, ul), grad) - beta * gamma * sk * product3((xh, xl), state)
    for i in range(TILES):
        bi, upto, onward = band(i), slice(0, (i + 1) * TILE), slice(i * TILE, SPAN)
        m.dirs[0, bi] = dq[bi] + product2l((m.fqh[bi, upto], m.fql[bi, upto]), kr[upto])
        part = product2l((m.fqh[onward, bi], m.fql[onward, bi]), qr[onward], (0, 0))
        part = part + product2l((m.fkh[onward, bi], m.fkl[onward, bi]), kr[onward], (0, 0))
        part = part + product2l((m.fkh[bi, upto], m.fkl[bi, upto]), kr[upto])
        m.dirs[1, bi] = dk[bi] + part
    send_directions()
    qf, kf = qr.astype(F32), kr.astype(F32)
    after = product3(state, halves(phit)) + bt
    total = jnp.sum(jnp.sum(grad_t * after, axis=1, keepdims=True), axis=0, keepdims=True)
    xu = jnp.sum(x * u, axis=1, keepdims=True)
    change = jnp.sum(
        qf * m.dirs[0] - kf * m.dirs[1] - 2.0 * (vr.astype(F32) * dv), axis=1, keepdims=True
    )
    change = change + 2.0 * xu
    change = jnp.where(iota((SPAN, 1), 0) == SPAN - 1, change + total, change)
    lane, row = iota((SPAN, TILE), 1), iota((SPAN, TILE), 0)
    pieces = [p.astype(F32) for p in thirds(jnp.broadcast_to(change, (SPAN, TILE)))]
    packed = jnp.zeros((SPAN, TILE), F32)
    for n in range(3):
        packed = jnp.where(lane == n, pieces[n], packed)
    ddecay = -jnp.sum(product(m.upper[...], packed.astype(BF16)), axis=1, keepdims=True)
    ddecay = jnp.broadcast_to(ddecay, (SPAN, TILE))
    out = jnp.where(lane == row % ROWS, xu * (1.0 - beta), 0.0)
    out = jnp.where(lane == row % ROWS + ROWS, ddecay, out)
    high, middle, low = thirds(out)
    fold = m.fold[...]
    lines = product(fold, high) + product(fold, middle) + product(fold, low)
    send_rows(lines)
    finish_directions(qf, kf)


class Memory:
    def __init__(self, **refs):
        self.__dict__.update(refs)


def scratch():
    dma = pltpu.SemaphoreType.DMA
    square, tall, big = (TILE, TILE), (SPAN, TILE), (SPAN, SPAN)
    part, lines, double = (HEADS, ROWS, TILE), (HEADS, 1, TILE), (2 * TILE, TILE)
    shapes = dict(
        columns=((TILE, TILE), F32),
        lower=(big, BF16), upper=(big, BF16), fold=((HEADS, SPAN), BF16), unfold=((SPAN, HEADS), BF16),
        start=(tall, jnp.int32), end=(tall, F32), weight=(tall, F32),
        beta=(tall, F32), gamma=(tall, F32), sk=(tall, F32), csw=(tall, F32),
        u0=(tall, F32), wk=(tall, F32), x0=(tall, F32), xk=(tall, F32),
        gqk=(big, F32), gkk=(big, F32), a=(big, F32),
        th=(big, BF16), tl=(big, BF16), ph=(big, BF16), pl=(big, BF16),
        fqh=(big, BF16), fql=(big, BF16), fkh=(big, BF16), fkl=(big, BF16),
        zh=((SPAN, 2 * TILE), BF16), zl=((SPAN, 2 * TILE), BF16),
        dirs=((2,) + tall, F32), partner=(tall, F32),
        maps_out=((2,) + double, F32), maps_in=((2,) + double, F32),
        far_out=((2, 3) + square, F32), far_in=((2, 4) + square, F32),
        q_here=((ROWS, HEADS * TILE // 2), BF16), k_here=((ROWS, HEADS * TILE // 2), BF16),
        v_here=((ROWS, HEADS * TILE), BF16), g_here=((ROWS, HEADS * TILE), BF16),
        beta_here=((ROWS, HEADS), F32), decay_here=((ROWS, HEADS), F32),
        ratio_here=((1, ROWS), F32), clip_here=((1, ROWS), jnp.int32),
    )
    for name in "kqvgdp":
        shapes[name + "_out"] = (part, BF16)
        shapes[name + "_in"] = (part, BF16)
    for name in ("rows", "back"):
        shapes[name + "_out"] = (lines, F32)
        shapes[name + "_in"] = (lines, F32)
    memory = {name: pltpu.VMEM(*shape) for name, shape in shapes.items()}
    memory.update(
        plane_send=dma((8,)), plane_recv=dma((8,)), map_send=dma((2, 2 + 4 * CHUNKS)), map_recv=dma((2, 2 + 4 * CHUNKS)),
        pair_send=dma((TILES,)), pair_recv=dma((TILES,)), here=dma((8,)),
    )
    return memory


def whole(
    q_ref, k_ref, v_ref, g_ref, beta_ref, decay_ref, ratio_ref, clip_ref, lengths_ref,
    dirs_ref, values_ref, lines_ref, *refs,
):
    m = Memory(**dict(zip(scratch(), refs)))
    dp, head, me, device = place()
    count, core = lax.axis_size("dp"), lax.rem(head, 2)

    def along(distance):
        return (lax.rem(dp + (count + 4 * distance), count), head)

    barrier = greet_plane(me, device)
    for distance in REACH:
        for sign in (1, -1):
            pl.semaphore_signal(
                barrier, inc=1, device_id=along(sign * distance), device_id_type=MESH
            )

    names = ("k", "beta", "decay", "ratio", "clip", "v", "q", "g")
    sources = (k_ref, beta_ref, decay_ref, ratio_ref, clip_ref, v_ref, q_ref, g_ref)
    local = {}
    for n, (name, source) in enumerate(zip(names, sources)):
        local[name] = pltpu.make_async_copy(source, getattr(m, name + "_here"), m.here.at[n])
        local[name].start()

    kinds = (("k", "rows"), ("v",), ("q", "g"), ("d",), ("back",), ("p",))
    number = {name: n for n, name in enumerate(n for kind in kinds for n in kind)}

    def kind_of(index):
        return [
            (getattr(m, n + "_out"), getattr(m, n + "_in"), m.plane_send.at[number[n]], m.plane_recv.at[number[n]])
            for n in kinds[index]
        ]

    m.columns[...] = jnp.zeros((TILE, TILE), F32)
    for name in names[:5]:
        local[name].wait()
    m.columns[0:ROWS, 0:HEADS] = m.beta_here[...]
    m.columns[ROWS : 2 * ROWS, 0:HEADS] = m.decay_here[...]
    weight = m.ratio_here[...] * m.clip_here[...].astype(F32)
    turned = jnp.transpose(m.columns[...])[0:HEADS]
    m.columns[0:HEADS, :] = turned
    m.columns[0:HEADS, 2 * ROWS : 3 * ROWS] = jnp.broadcast_to(weight, (HEADS, ROWS))
    for j in range(HEADS):
        m.k_out[j] = m.k_here[:, band(j // 2)]
        m.rows_out[j] = m.columns[j : j + 1, :]
    pl.semaphore_wait(barrier, HEADS - 1 + 2 * len(REACH))
    start_plane(me, device, kind_of(0))
    local["v"].wait()
    for j in range(HEADS):
        m.v_out[j] = m.v_here[:, band(j)]
    await_sent(kind_of(0))
    start_plane(me, device, kind_of(1))
    prepare(lax.div(dp, 4) * SPAN, lengths_ref, m)
    local["q"].wait()
    local["g"].wait()
    for j in range(HEADS):
        m.q_out[j] = m.q_here[:, band(j // 2)]
        m.g_out[j] = m.g_here[:, band(j)]
    await_sent(kind_of(1))
    start_plane(me, device, kind_of(2))
    await_landed(kind_of(0))
    first_keys(m)
    await_landed(kind_of(1))

    copies = {}

    def ship(way, slot, source, target, distance):
        copies[way, slot] = pltpu.make_async_remote_copy(
            src_ref=source,
            dst_ref=target,
            send_sem=m.map_send.at[way, slot],
            recv_sem=m.map_recv.at[way, slot],
            device_id=along(distance if way == 0 else -distance),
            device_id_type=MESH,
        )
        copies[way, slot].start()

    def ship_half(way, half, value):
        rows = pl.ds(half * TILE, TILE)
        m.maps_out[way, rows] = value
        ship(way, half, m.maps_out.at[way, rows], m.maps_in.at[way, rows], 1)

    def ship_chunk(way, level, chunk, source):
        rows = pl.ds(chunk * (TILE // CHUNKS), TILE // CHUNKS)
        ship(way, 2 + level * CHUNKS + chunk, source.at[rows], m.far_in.at[way, level, rows], 2)

    def ship_bias(way, value):
        ship_half(way, 1, value)
        for chunk in range(CHUNKS):
            ship_chunk(way, 0, chunk, m.maps_out.at[way, pl.ds(TILE, TILE)])

    phit, bt = first_state(m)
    ship_half(0, 0, phit)
    ship_half(1, 0, jnp.transpose(phit))
    ship_bias(0, bt)
    await_landed(kind_of(2))
    lt = first_grad(m)
    ship_bias(1, lt)
    first_beside(m)
    near, steps, biases = [], [], []
    for way in range(2):
        copies[way, 0].wait_recv()
        near.append(halves(m.maps_in[way, 0:TILE]))
        own = halves(m.maps_out[way, 0:TILE])
        steps.append(halves(product3(near[way], own)))
    for way in range(2):
        copies[way, 1].wait_recv()
        own = halves(m.maps_out[way, 0:TILE])
        biases.append(product3(halves(m.maps_in[way, TILE:]), own) + m.maps_out[way, TILE:])
    ends = [[], []]
    for level in range(4):
        for chunk in range(CHUNKS):
            rows = band(chunk, TILE // CHUNKS)
            for way in range(2):
                copies[way, 2 + level * CHUNKS + chunk].wait_recv()
                arrived = halves(m.far_in[way, level, rows])
                if level < 3:
                    m.far_out[way, level, rows] = product3(arrived, steps[way]) + biases[way][rows]
                    ship_chunk(way, level + 1, chunk, m.far_out.at[way, level])
                else:
                    bias = m.maps_in[way, TILE + chunk * (TILE // CHUNKS) :][: TILE // CHUNKS]
                    ends[way].append(product3(arrived, near[way]) + bias)
    ends = [joined(pieces, 0) for pieces in ends]

    def send_values(dv):
        m.d_out[...] = dv.astype(BF16).reshape(HEADS, ROWS, TILE)
        start_plane(me, device, kind_of(3))

    pairs = []

    def send_directions():
        pairs.append(
            pltpu.make_async_remote_copy(
                src_ref=m.dirs.at[1 - core],
                dst_ref=m.partner,
                send_sem=m.pair_send.at[0],
                recv_sem=m.pair_recv.at[0],
                device_id=(dp, head + 1 - 2 * core),
                device_id_type=MESH,
            )
        )
        pairs[-1].start()

    def finish_directions(qf, kf):
        own = jnp.where(core == 0, qf, kf)
        inverse = 1.0 / (jnp.sum(own * own, axis=1, keepdims=True) + 1e-06)
        for pair in pairs:
            pair.wait_recv()
        part = m.dirs[core] + m.partner[...]
        part = part - own * (jnp.sum(own * part, axis=1, keepdims=True) * inverse)
        m.p_out[...] = part.astype(BF16).reshape(HEADS, ROWS, TILE)
        start_plane(me, device, kind_of(5))

    def send_rows(lines):
        for j in range(HEADS):
            m.back_out[j] = lines[j : j + 1, :]
        start_plane(me, device, kind_of(4))

    second(
        m, ends[0], ends[1], phit, bt, send_values, send_directions, finish_directions, send_rows
    )
    for one in list(copies.values()) + pairs:
        one.wait_send()
    for index in (2, 3, 4, 5):
        await_sent(kind_of(index))
    await_landed(kind_of(3))
    values_ref[...] = m.d_in[...]
    await_landed(kind_of(5))
    dirs_ref[...] = m.p_in[...]
    await_landed(kind_of(4))
    lines_ref[...] = m.back_in[...]


def unpack(dirs_ref, values_ref, lines_ref, dq_ref, dk_ref, dv_ref, db_ref, dd_ref):
    for j in range(HEADS):
        to_ref = (dq_ref, dk_ref)[j % 2]
        to_ref[:, band(j // 2)] = dirs_ref[j]
        dv_ref[:, band(j)] = values_ref[j]
    lines = joined([lines_ref[:, 0, :], jnp.zeros((TILE - HEADS, TILE), F32)], 0)
    turned = jnp.transpose(lines)
    db_ref[...] = turned[0:ROWS, 0:HEADS]
    dd_ref[...] = turned[ROWS : 2 * ROWS, 0:HEADS]


def shards(query, key, value, beta_logit, decay, out_grad, ratio, clip_mask, lengths):
    vmem, smem = [pl.BlockSpec(memory_space=m) for m in (pltpu.VMEM, pltpu.SMEM)]
    part, lines = (HEADS, ROWS, TILE), (HEADS, 1, TILE)
    blocks = pl.pallas_call(
        whole,
        out_shape=[jax.ShapeDtypeStruct(s, d) for s, d in ((part, BF16), (part, BF16), (lines, F32))],
        in_specs=[pl.BlockSpec(memory_space=pl.ANY)] * 8 + [smem],
        out_specs=[vmem] * 3,
        scratch_shapes=list(scratch().values()),
        compiler_params=pltpu.CompilerParams(
            vmem_limit_bytes=LIMIT, collective_id=0, has_side_effects=True
        ),
        cost_estimate=pl.CostEstimate(flops=1 << 30, bytes_accessed=1 << 20, transcendentals=0),
        name="whole",
    )(
        query, key, value, out_grad, beta_logit, decay,
        ratio.reshape(1, ROWS), clip_mask.reshape(1, ROWS), lengths,
    )
    wide = HEADS * HEAD_DIM
    shapes = [((ROWS, wide // 2), BF16)] * 2 + [((ROWS, wide), BF16)] + [((ROWS, HEADS), F32)] * 2
    return tuple(
        pl.pallas_call(
            unpack,
            out_shape=[jax.ShapeDtypeStruct(s, d) for s, d in shapes],
            in_specs=[vmem] * 3,
            out_specs=[vmem] * 5,
            compiler_params=pltpu.CompilerParams(vmem_limit_bytes=LIMIT),
            cost_estimate=pl.CostEstimate(flops=0, bytes_accessed=1 << 20, transcendentals=0),
            name="unpack",
        )(*blocks)
    )


def solution(mesh):
    split = P(("dp", "head"), None)
    line = P(("dp", "head"))
    return jax.shard_map(
        shards,
        mesh=mesh,
        in_specs=(split,) * 6 + (line, line, P()),
        out_specs=(split,) * 5,
        check_vma=False,
    )
```

time: 1110 us -> 64.6 us (0.06)
  the two profiles are of different devices: /device:TPU:250 before, /device:TPU:1 now
where the time goes in v3:
time: 64.6 us; the launch traced here: 64.5 us
  Pallas kernels  63.8 us (99%)
    pallas_call x1, Pallas kernels, shards(): pl.pallas_call(whole, out_shape=[jax.ShapeDtypeStruct(s, d) for s, d in (...  62.1 us
    pallas_call x1, Pallas kernels, shards(): pl.pallas_call(unpack, out_shape=[jax.ShapeDtypeStruct(s, d) for s, d in...  1.69 us

profile of v3, /device:TPU:1, one launch (start us, length us, event | category | flops | bytes accessed | tf_op | source)
XLA Modules:
  0.0 64.5 jit_solution(10198339914983218137)
XLA Ops:
  0.6 62.1 %whole.1 = (bf16[32,16,128]{2,1,0:T(8,128)(2,1)}, bf16[32,16,128]{2,1,0:T(8,128)(2,1)}, f32[32,1,128]{2,1,0:T(1,128)}) custom-call(bf16[16,2048]{1,0:T(8,128)(2,1)} %q_ref.1, bf16[16,2048]{1,0:T(8,128)(2,1)} %k_ref.1, bf16[16,4096]{1,0:T(8,128)(2,1)} %v_ref.1, bf16[16,4096]{1,0:T(8,128)(2,1)} %g_ref.1, f32[16,32]{1,0:T(8,128)} %beta_ref.1, ...), custom_call_target="tpu_custom_call" | custom-call | flops 1073741824 | bytes 1048576 | tf_op jit(solution)/shard_map/whole/pallas_call | solution.py:545
  62.8 1.7 %unpack.1 = (bf16[16,2048]{1,0:T(8,128)(2,1)}, bf16[16,2048]{1,0:T(8,128)(2,1)}, bf16[16,4096]{1,0:T(8,128)(2,1)}, f32[16,32]{1,0:T(8,128)}, f32[16,32]{1,0:T(8,128)}) custom-call(bf16[32,16,128]{2,1,0:T(8,128)(2,1)} %get-tuple-element.8.dirs_ref, bf16[32,16,128]{2,1,0:T(8,128)(2,1)} %get-tuple-element.9.values_ref, f32[32,1,128]{2,1,0:T(1,128)} %get-tuple-element.10.lines_ref), custom_call_target="tpu_custom_call" | custom-call | bytes 1048576 | tf_op jit(solution)/shard_map/unpack/pallas_call | solution.py:563
